TPU v7x, 32 devices: a whole 2x2x4 slice. The times are simulated.
32 devices in a mesh: groups: 2 (over y), leaf: 16 (over z, x, core).
Axes of the slice: x: 2, y: 2, z: 4, core: 2. Of those that a mesh axis runs over, the one named last changes fastest.
Arguments:
- points: float32 [32, 262144], P(None, ('groups', 'leaf')), parts along dimension 1, may hold values from -6 to 6
- solution: float32 [262144], P(('groups', 'leaf')), parts along dimension 0, may hold values from -6 to 6
- residual: float32 [262144], P(('groups', 'leaf')), parts along dimension 0
- direction: float32 [262144], P(('groups', 'leaf')), parts along dimension 0
- ridge_weight: float32 [2], P('groups'), parts along dimension 0, may hold values from 0.5 to 2
- kernel_rate: float32 [2], P('groups'), parts along dimension 0, may hold values from 0.0390625 to 0.0625
- tree_perm: int32 [32, 8192], P(('groups', 'leaf')), parts along dimension 0, may hold values from 0 to 8191, each once within a row
- local_skeleton: float32 [1984, 32, 256], P(('groups', 'leaf')), parts along dimension 0, may hold values from -6 to 6
- local_transfer: bfloat16 [1984, 256, 256], P(('groups', 'leaf')), parts along dimension 0, may hold values from -0.375 to 0.375
- cross_skeleton: float32 [128, 2, 32, 256], P(('groups', 'leaf')), parts along dimension 0, as said below
- cross_transfer: bfloat16 [96, 2, 256, 256], P(('groups', 'leaf')), parts along dimension 0, as said below
- near_target: int32 [8192], P(('groups', 'leaf')), parts along dimension 0, may hold values from 0 to 511, as said below
- near_source: int32 [8192], P(('groups', 'leaf')), parts along dimension 0, may hold values from 0 to 511, as said below
- tile_count: int32 [32], P(('groups', 'leaf')), parts along dimension 0, may hold values from 64 to 256, as said below
Outputs:
- new_solution: float32 [262144], P(('groups', 'leaf')), parts along dimension 0
- new_residual: float32 [262144], P(('groups', 'leaf')), parts along dimension 0
- new_direction: float32 [262144], P(('groups', 'leaf')), parts along dimension 0
There are 2 independent parts, one for each index of `groups`. A program takes and returns all parts, laid end to end along the dimension named above; each array names one. Nothing has to cross between parts.
Inputs may be any that keep to these rules, and one draw needn't show every extreme that they name: `tree_perm`: each row is a permutation of the device's 8192 positions. `near_target`: slot s of device d is a leaf of device d; its first 32 slots name its leaves in order and pair them with themselves. A pair listed twice counts twice. `near_source`: A source lies at most 16 leaves from its target in tree order, within the leaves of the problem; every device has a live pair at distance exactly 16 on each side or mirrored at an end. `tile_count`: slots at or past a device's count are not part of the operator. `cross_skeleton`: entries for level l are equal on all devices with the same level l ancestor; member 1 equals member 0 of the devices of the sibling. `cross_transfer`: entries for level l are equal on all devices with the same level l ancestor; member 1 equals member 0 of the devices of the sibling.
All inputs are finite; a program needn't handle non-finite values.
Results may differ from a plain program's by a relative error of at most 0.0003.
Values sent between devices are 32-bit elements; how exact they have to be, the bound alone decides.
A program may use at most 128 MiB of HBM per device.

v0:
```python
import jax
import jax.numpy as jnp
from jax import lax
from jax.sharding import PartitionSpec as P

LEAF = 256
LEAVES_DEV = 32


epsilon = 1e-06
half_root = 0.5**0.5


def extended_2(array, sides, width):
    for axis, dim in sides:
        devices, length = (lax.axis_size(axis), array.shape[dim])
        up = [(i, (i + 1) % devices) for i in range(devices - 1)]
        down = [(j, i) for i, j in up]
        last = lax.slice_in_dim(array, length - width, length, axis=dim)
        first = lax.slice_in_dim(array, 0, width, axis=dim)
        before = lax.ppermute(last, axis, up)
        after = lax.ppermute(first, axis, down)
        array = jnp.concatenate([before, array, after], axis=dim)
    return array


def partner(value, axis, distance):
    mask = 2**distance
    pairs = [(source, source ^ mask) for source in range(lax.axis_size(axis))]
    return lax.ppermute(value, axis, pairs)


def kernel_block(first_set, second_set, rate_value):
    first_norms = jnp.sum(first_set * first_set, axis=-2)
    second_norms = jnp.sum(second_set * second_set, axis=-2)
    inner_prod = jnp.einsum(
        "...dm,...dn->...mn", first_set, second_set, precision=lax.Precision.HIGHEST
    )
    distance = first_norms[..., :, None] + second_norms[..., None, :] - 2.0 * inner_prod
    return jnp.exp(-rate_value * distance)


def local_tree(tree_points, tree_dir, skeleton, transfer, rate_value):
    leaves_here = tree_points.shape[0]
    leaf_kernel = kernel_block(skeleton[:leaves_here], tree_points, rate_value)
    upward_list = [jnp.einsum("lrp,lp->lr", leaf_kernel, tree_dir, precision=lax.Precision.HIGHEST)]
    coupled = []
    offset = 0
    width_now = leaves_here
    while width_now >= 2:
        node_skeleton = skeleton[offset : offset + width_now]
        flipped = jnp.flip(
            node_skeleton.reshape((width_now // 2, 2) + node_skeleton.shape[1:]), axis=1
        ).reshape(node_skeleton.shape)
        values_flipped = jnp.flip(upward_list[-1].reshape(width_now // 2, 2, -1), axis=1).reshape(
            width_now, -1
        )
        couple_kernel = kernel_block(node_skeleton, flipped, rate_value)
        coupled.append(
            jnp.einsum("nrs,ns->nr", couple_kernel, values_flipped, precision=lax.Precision.HIGHEST)
        )
        lifted = jnp.einsum(
            "nrs,nr->ns",
            transfer[offset : offset + width_now].astype(jnp.float32),
            upward_list[-1],
            precision=lax.Precision.HIGHEST,
        )
        upward_list.append((lifted[0::2] + lifted[1::2]) * half_root)
        offset = offset + width_now
        width_now = width_now // 2
    return (leaf_kernel, upward_list[-1][0], coupled)


def local_down(root_value, transfer, coupled):
    spans = []
    offset = 0
    for portion in coupled:
        spans.append((offset, portion.shape[0]))
        offset = offset + portion.shape[0]
    downward = root_value[None, :]
    for position in range(len(coupled) - 1, -1, -1):
        first_node, width_now = spans[position]
        parent = jnp.repeat(downward, 2, axis=0)
        downward = coupled[position] + jnp.einsum(
            "nrs,ns->nr",
            transfer[first_node : first_node + width_now].astype(jnp.float32),
            parent,
            precision=lax.Precision.HIGHEST,
        )
    return downward


def near_field(
    tree_points, extended, near_target, near_source, tile_total, first_leaf, own_first, rate_value
):
    dims = tree_points.shape[1]
    leaves_here = tree_points.shape[0]

    def tile_block(block_id, running):
        slot_ids = block_id * 8 + jnp.arange(8, dtype=jnp.int32)
        target_rows = lax.dynamic_slice_in_dim(near_target, block_id * 8, 8) - own_first
        source_rows = lax.dynamic_slice_in_dim(near_source, block_id * 8, 8) - first_leaf
        alive_mask = (slot_ids < tile_total).astype(jnp.float32)
        target_pts = tree_points[target_rows]
        source_pack = extended[source_rows]
        block_kernel = kernel_block(target_pts, source_pack[:, :dims], rate_value)
        portion = (
            jnp.einsum(
                "bij,bj->bi", block_kernel, source_pack[:, dims], precision=lax.Precision.HIGHEST
            )
            * alive_mask[:, None]
        )
        target_hot = (
            target_rows[:, None] == jnp.arange(leaves_here, dtype=jnp.int32)[None, :]
        ).astype(jnp.float32)
        return running + jnp.einsum(
            "bl,bi->li", target_hot, portion, precision=lax.Precision.HIGHEST
        )

    blocks = (tile_total + 7) // 8
    return lax.fori_loop(
        0, blocks, tile_block, jnp.zeros((leaves_here, tree_points.shape[2]), jnp.float32)
    )


def shards(
    points,
    solution,
    residual,
    direction,
    ridge_weight,
    kernel_rate,
    tree_perm,
    local_skeleton,
    local_transfer,
    cross_skeleton,
    cross_transfer,
    near_target,
    near_source,
    tile_count,
):
    rate_value = kernel_rate[0]
    tree_order = tree_perm[0]
    leaves_here = LEAVES_DEV
    dims = points.shape[0]
    tree_points = jnp.transpose(points[:, tree_order].reshape(dims, leaves_here, LEAF), (1, 0, 2))
    tree_dir = direction[tree_order].reshape(leaves_here, LEAF)
    packed = jnp.concatenate([tree_points, tree_dir[:, None, :]], axis=1)
    extended = extended_2(packed, (("leaf", 0),), leaves_here)
    device_index = lax.axis_index("leaf")
    own_first = device_index * leaves_here
    leaf_kernel, root_value, coupled = local_tree(
        tree_points, tree_dir, local_skeleton, local_transfer, rate_value
    )
    levels = lax.axis_size("leaf").bit_length() - 1
    couple_kernel = kernel_block(cross_skeleton[:, 0], cross_skeleton[:, 1], rate_value)
    own_transfer = cross_transfer[:, 0].astype(jnp.float32)
    current = root_value
    sibling_list = []
    for level in range(levels):
        sibling_value = partner(current, "leaf", level)
        sibling_list.append(sibling_value)
        if level < levels - 1:
            mine_lift = jnp.dot(current, own_transfer[level], precision=lax.Precision.HIGHEST)
            other_lift = jnp.dot(
                sibling_value,
                cross_transfer[level, 1].astype(jnp.float32),
                precision=lax.Precision.HIGHEST,
            )
            current = (mine_lift + other_lift) * half_root
    sibling_values = jnp.stack(sibling_list)
    cross_values = jnp.einsum(
        "lrs,ls->lr", couple_kernel, sibling_values, precision=lax.Precision.HIGHEST
    )
    current = cross_values[levels - 1]
    for level in range(levels - 2, -1, -1):
        current = cross_values[level] + jnp.dot(
            own_transfer[level], current, precision=lax.Precision.HIGHEST
        )
    near = near_field(
        tree_points,
        extended,
        near_target,
        near_source,
        tile_count[0],
        own_first - leaves_here,
        own_first,
        rate_value,
    )
    downward = local_down(current, local_transfer, coupled)
    far = jnp.einsum("lrp,lr->lp", leaf_kernel, downward, precision=lax.Precision.HIGHEST)
    image_tree = ridge_weight[0] * tree_dir + near + far
    image = jnp.zeros(residual.shape, jnp.float32).at[tree_order].set(image_tree.reshape(-1))
    norm_old, curvature = lax.psum(
        (jnp.sum(residual * residual), jnp.sum(direction * image)), "leaf"
    )
    step_size = norm_old / curvature
    new_residual = residual - step_size * image
    norm_new = lax.psum(jnp.sum(new_residual * new_residual), "leaf")
    new_solution = solution + step_size * direction
    new_direction = new_residual + norm_new / (norm_old + epsilon) * direction
    return (new_solution, new_residual, new_direction)


def solution(mesh):
    return jax.shard_map(
        shards,
        mesh=mesh,
        in_specs=(
            P(None, ("groups", "leaf")),
            P(("groups", "leaf")),
            P(("groups", "leaf")),
            P(("groups", "leaf")),
            P("groups"),
            P("groups"),
            P(("groups", "leaf"), None),
            P(("groups", "leaf"), None, None),
            P(("groups", "leaf"), None, None),
            P(("groups", "leaf"), None, None, None),
            P(("groups", "leaf"), None, None, None),
            P(("groups", "leaf")),
            P(("groups", "leaf")),
            P(("groups", "leaf")),
        ),
        out_specs=(P(("groups", "leaf")), P(("groups", "leaf")), P(("groups", "leaf"))),
        check_vma=False,
    )
```

profile of v0, /device:TPU:0, one launch (start us, length us, event | category | flops | bytes accessed | tf_op | source)
XLA Modules:
  0.0 610.4 jit_solution(15260435448366767813)
XLA Ops:
  2.1 45.5 %gather_fusion.2 = f32[8192]{0:T(1024)S(1)} fusion(f32[8192]{0:T(1024)S(1)} %copy-done, s32[8192]{0:T(1024)S(1)} %broadcast_clamp_fusion), kind=kCustom, calls=%fused_computation.2 | custom fusion | bytes 98304 | tf_op jit(solution)/shard_map/gather | solution.py:147
  50.3 29.9 %gather_fusion.3 = f32[8192,32]{1,0:T(8,128)} fusion(f32[32,8192]{0,1:T(8,128)} %copy.23, s32[8192]{0:T(1024)S(1)} %broadcast_clamp_fusion), kind=kCustom, calls=%fused_computation.3 | custom fusion | bytes 2129920 | tf_op jit(solution)/shard_map/gather | solution.py:146
  80.2 3.0 copy.24
  85.8 4.0 collective-permute-start
  92.2 8.1 %fusion.145 = f32[32,256,256]{2,1,0:T(8,128)S(1)} fusion(f32[32,32,256]{1,2,0:T(8,128)S(1)} %bitcast.212, f32[62,32,256]{2,1,0:T(8,128)} %param.23), kind=kOutput, calls=%fused_computation.212 | convolution fusion | flops 805306368 | bytes 10485760 | tf_op jit(solution)/shard_map/...dm,...dn->...mn/dot_general | solution.py:36
  100.4 7.1 %fusion.26 = f32[32,1,256]{2,1,0:T(1,128)S(1)} fusion(f32[32,256,1]{1,2,0:T(1,128)S(1)} %bitcast.229, f32[32,256,256]{2,1,0:T(8,128)S(1)} %fusion.145, f32[32,256]{1,0:T(8,128)S(1)} %multiply_reduce_fusion.3, f32[32,256]{1,0:T(8,128)S(1)} %get-tuple-element.179, f32[]{:T(128)} %bitcast.6), kind=kOutput, calls=%fused_computation.43 | convolution fusion | flops 33554432 | bytes 8519684 | tf_op jit(solution)/shard_map/lrp,lp->lr/dot_general | solution.py:46
  141.3 4.3 fusion.152
  145.5 8.9 %fusion.151 = f32[16,256,256]{2,1,0:T(8,128)} fusion(f32[62,32,256]{2,1,0:T(8,128)S(1)} %copy-done.3, f32[16,32,256]{2,1,0:T(8,128)S(1)} %bitcast.226), kind=kOutput, calls=%fused_computation.218 | convolution fusion | flops 402653184 | bytes 6750208 | tf_op jit(solution)/shard_map/...dm,...dn->...mn/dot_general | solution.py:36
  160.2 8.0 %fusion.150 = f32[32,256,256]{1,2,0:T(8,128)S(1)} fusion(f32[62,32,256]{2,1,0:T(8,128)S(1)} %copy-done.3, f32[32,32,256]{2,1,0:T(8,128)} %bitcast.225), kind=kOutput, calls=%fused_computation.217 | convolution fusion | flops 805306368 | bytes 11468800 | tf_op jit(solution)/shard_map/...dm,...dn->...mn/dot_general | solution.py:36
  174.0 6.9 %fusion.18 = f32[32,1,256]{2,1,0:T(1,128)S(1)} fusion(f32[32,256,1]{1,2,0:T(1,128)S(1)} %copy-done.20, f32[32,256,256]{1,2,0:T(8,128)S(1)} %fusion.150, f32[32,256]{1,0:T(8,128)S(1)} %add.246, f32[32,256]{1,0:T(8,128)S(1)} %copy-done.16, f32[]{:T(128)} %bitcast.6), kind=kOutput, calls=%fused_computation.36 | convolution fusion | flops 33554432 | bytes 8519684 | tf_op jit(solution)/shard_map/nrs,ns->nr/dot_general | solution.py:60
  183.2 4.6 fusion.30
  189.5 2.8 copy.25
  214.3 3.3 fusion.60
  217.7 5.5 fusion.46
  223.2 11.4 %fusion.24 = f32[32,1,256]{2,1,0:T(1,128)S(1)} fusion(f32[32,256,256]{2,1,0:T(8,128)} %copy-done.2, f32[32,256]{1,0:T(8,128)S(1)} %copy-done.19, f32[32,256]{1,0:T(8,128)S(1)} %copy-done.16, f32[]{:T(128)} %bitcast.6, f32[32,256,1]{1,0,2:T(8,128)S(1)} %fusion.123), kind=kOutput, calls=%fused_computation.42 | convolution fusion | flops 33554432 | bytes 8519684 | tf_op jit(solution)/shard_map/lrp,lr->lp/dot_general | solution.py:191
  236.4 3.8 copy.26
  240.2 137.3 %while.12 = (s32[]{:T(128)}, f32[32,256]{1,0:T(8,128)S(1)}, s32[]{:T(128)}, s32[256]{0:T(256)S(1)}, s32[]{:T(128)}, /*index=5*/f32[]{:T(128)}, f32[32,32,256]{2,...) while((s32[]{:T(128)}, f32[32,256]{1,0:T(8,128)S(1)}, ...), condition=%wide.region_5.6_spmd, body=%wide.region_2.0_spmd.sunk | while | flops 210772320 | bytes 6439507 | solution.py:121
  258.8 2.7 gather_fusion.1
  267.4 2.7 gather_fusion.1
  276.0 2.7 gather_fusion.1
  284.6 2.7 gather_fusion.1
  377.6 30.6 %scatter_custom_fusion = f32[8192]{0:T(1024)S(1)} fusion(s32[8192]{0:T(1024)} %bitcast.234, f32[8192]{0:T(1024)S(1)} %bitcast.241, f32[]{:T(128)} %constant.69.clone.1), kind=kCustom, calls=%fused_computation.177 | custom fusion | bytes 33280 | tf_op jit(solution)/shard_map/scatter | solution.py:193
  408.9 166.7 %all-reduce = (f32[]{:T(128)}, f32[]{:T(128)}) all-reduce(f32[]{:T(128)} %get-tuple-element.196, f32[]{:T(128)} %get-tuple-element.195), channel_id=1, replica_groups=mesh['groups'=2,'leaf'=16] {'leaf'}, use_global_device_ids=true, to_apply=%region_1.0 | all-reduce | flops 2 | bytes 16 | tf_op jit(solution)/shard_map/psum | solution.py:194
  578.2 30.4 %psum.23 = f32[]{:T(128)} all-reduce(f32[]{:T(128)} %get-tuple-element.173), channel_id=1, replica_groups=mesh['groups'=2,'leaf'=16] {'leaf'}, use_global_device_ids=true, to_apply=%region_23.24 | all-reduce | flops 1 | bytes 8 | tf_op jit(solution)/shard_map/psum | solution.py:199
  (378 shorter events, 206.7 us)
Async XLA Ops:
  2.1 45.6 %copy-start.5 = (f32[32,8192]{1,0:T(8,128)S(1)}, f32[32,8192]{1,0:T(8,128)}, u32[]{:S(2)}) copy-start(f32[32,8192]{1,0:T(8,128)} %param.16) | copy-start | bytes 3145732
  84.4 150.2 %collective-permute-start.1 = (f32[32,33,256]{2,0,1:T(8,128)}, f32[32,33,256]{2,0,1:T(8,128)}, u32[]{:S(2)}, u32[]{:S(2)}) collective-permute-start(f32[32,33,256]{2,0,1:T(8,128)} %pad_maximum_fusion.1), channel_id=1, source_target_pairs={{1,0},{2,1},{3,2},{4,3},{5,4},{6,5},{7,6},{8,7},{9,8},{10,9},{11,1... | collective-permute-start | bytes 3244040 | tf_op jit(solution)/shard_map/ppermute | solution.py:22
  85.8 148.8 %collective-permute-start = (f32[32,33,256]{2,0,1:T(8,128)}, f32[32,33,256]{2,0,1:T(8,128)}, u32[]{:S(2)}, u32[]{:S(2)}) collective-permute-start(f32[32,33,256]{2,0,1:T(8,128)} %pad_maximum_fusion.1), channel_id=1, source_target_pairs={{0,1},{1,2},{2,3},{3,4},{4,5},{5,6},{6,7},{7,8},{8,9},{9,10},{10,1... | collective-permute-start | bytes 3244040 | tf_op jit(solution)/shard_map/ppermute | solution.py:21
  89.9 10.5 %copy-start.18 = (f32[32,256]{1,0:T(8,128)}, f32[32,256]{1,0:T(8,128)S(1)}, u32[]{:S(2)}) copy-start(f32[32,256]{1,0:T(8,128)S(1)} %multiply_reduce_fusion.3) | copy-start | bytes 98308
  90.6 16.9 %slice-start = ((s8[8126464]{0:T(1024)(128)(4,1)}), s8[4194304]{0:T(1024)(128)(4,1)S(1)}, s32[]{:S(2)}) async-start(s8[8126464]{0:T(1024)(128)(4,1)} %bitcast.213), calls=%async_computation | async-start | bytes 8388608
  92.2 15.3 %slice-start.1 = ((s8[8126464]{0:T(1024)(128)(4,1)}), s8[3932160]{0:T(1024)(128)(4,1)S(1)}, s32[]{:S(2)}) async-start(s8[8126464]{0:T(1024)(128)(4,1)} %bitcast.213), calls=%async_computation.1 | async-start | bytes 7864320
  115.7 19.6 %copy-start.7 = (f32[4,2,32,256]{3,2,1,0:T(8,128)S(1)}, f32[4,2,32,256]{3,2,1,0:T(8,128)}, u32[]{:S(2)}) copy-start(f32[4,2,32,256]{3,2,1,0:T(8,128)} %param.25) | copy-start | bytes 786436
  118.1 74.2 %collective-permute-start.2 = (f32[256]{0:T(256)}, f32[256]{0:T(256)}, u32[]{:S(2)}, u32[]{:S(2)}) collective-permute-start(f32[256]{0:T(256)} %bitcast.41), channel_id=1, source_target_pairs={{0,1},{1,0},{2,3},{3,2},{4,5},{5,4},{6,7},{7,6},{8,9},{9,8},{10,11... | collective-permute-start | bytes 3080 | tf_op jit(solution)/shard_map/ppermute | solution.py:30
  132.0 13.5 %copy-start.3 = (f32[62,32,256]{2,1,0:T(8,128)S(1)}, f32[62,32,256]{2,1,0:T(8,128)}, u32[]{:S(2)}) copy-start(f32[62,32,256]{2,1,0:T(8,128)} %param.23) | copy-start | bytes 6094852
  145.5 13.7 %copy-start.13 = (f32[8,2,256]{2,1,0:T(2,128)S(1)}, f32[8,2,256]{2,1,0:T(2,128)}, u32[]{:S(2)}) copy-start(f32[8,2,256]{2,1,0:T(2,128)} %reshape.163) | copy-start | bytes 49156
  160.1 11.0 %copy-start.26 = (f32[2,256,1]{1,0,2:T(2,128)S(1)}, f32[2,256,1]{1,0,2:T(2,128)}, u32[]{:S(2)}) copy-start(f32[2,256,1]{1,0,2:T(2,128)} %multiply_bitcast_fusion.1) | copy-start | bytes 6148
  160.2 11.6 %copy-start.10 = (f32[2,2,32,256]{3,2,1,0:T(8,128)S(1)}, f32[2,2,32,256]{3,2,1,0:T(8,128)}, u32[]{:S(2)}) copy-start(f32[2,2,32,256]{3,2,1,0:T(8,128)} %rev.42) | copy-start | bytes 393220
  160.2 11.6 %copy-start.31 = (f32[4,256]{1,0:T(4,128)S(1)}, f32[4,256]{1,0:T(4,128)}, u32[]{:S(2)}) copy-start(f32[4,256]{1,0:T(4,128)} %get-tuple-element.184) | copy-start | bytes 12292
  160.2 11.6 %copy-start.34 = (f32[4,256]{1,0:T(4,128)S(1)}, f32[4,256]{1,0:T(4,128)}, u32[]{:S(2)}) copy-start(f32[4,256]{1,0:T(4,128)} %add.260) | copy-start | bytes 12292
  174.0 9.3 %copy-start.21 = (f32[16,256]{1,0:T(8,128)S(1)}, f32[16,256]{1,0:T(8,128)}, u32[]{:S(2)}) copy-start(f32[16,256]{1,0:T(8,128)} %get-tuple-element.180) | copy-start | bytes 49156
  174.0 9.3 %copy-start.24 = (f32[16,256,1]{1,2,0:T(1,128)S(1)}, f32[16,256,1]{1,2,0:T(1,128)}, u32[]{:S(2)}) copy-start(f32[16,256,1]{1,2,0:T(1,128)} %reshape.284) | copy-start | bytes 49156
  174.0 9.3 %copy-start.38 = (f32[16,256,256]{2,1,0:T(8,128)S(1)}, f32[16,256,256]{2,1,0:T(8,128)}, u32[]{:S(2)}) copy-start(f32[16,256,256]{2,1,0:T(8,128)} %fusion.151) | copy-start | bytes 12582916
  193.1 4.0 collective-permute-start.3
  197.2 3.6 collective-permute-start.4
  201.0 4.5 collective-permute-start.5
  210.4 12.8 %copy-start.19 = (f32[32,256]{1,0:T(8,128)S(1)}, f32[32,256]{1,0:T(8,128)}, u32[]{:S(2)}) copy-start(f32[32,256]{1,0:T(8,128)} %copy-done.18) | copy-start | bytes 98308
  240.2 168.1 %copy-start.8 = (f32[8192]{0:T(1024)S(1)}, f32[8192]{0:T(1024)}, u32[]{:S(2)}) copy-start(f32[8192]{0:T(1024)} %param.18) | copy-start | bytes 98308
  240.2 369.1 %copy-start.17 = (f32[8192]{0:T(1024)S(1)}, f32[8192]{0:T(1024)}, u32[]{:S(2)}) copy-start(f32[8192]{0:T(1024)} %param.17) | copy-start | bytes 98308
  578.2 31.7 %copy-start.9 = (f32[8192]{0:T(1024)}, f32[8192]{0:T(1024)S(1)}, u32[]{:S(2)}) copy-start(f32[8192]{0:T(1024)S(1)} %get-tuple-element.174) | copy-start | bytes 98308
  (23 other events, 134.6 us)
where the time goes:
time: 617 us; the launch traced here: 610 us
  blocking collectives  197 us (32%)
  local copies, waits for them, and re-layouts  189 us (31%)
  matrix products  165 us (27%)
  other arithmetic  33.1 us (5%)
  starting transfers between devices  13.7 us (2%)
  between operations  6.58 us (1%)
    psum x1, blocking collectives, shards(): lax.psum((jnp.sum(residual * residual), jnp.sum(direction * image)), 'leaf')  167 us
    dot_general x23, matrix products, kernel_block(): jnp.einsum('...dm,...dn->...mn', first_set, second_set, precision=lax.Pre...  62.7 us
    gather x1, local copies, waits for them, and re-layouts, shards(): tree_dir = direction[tree_order].reshape(leaves_here, LEAF)  45.5 us
    gather x16, local copies, waits for them, and re-layouts, tile_block(): source_pack = extended[source_rows]  42.9 us
    dot_general x16, matrix products, tile_block(): jnp.einsum('bij,bj->bi', block_kernel, source_pack[:, dims], precision=la...  36.9 us
    scatter x1, local copies, waits for them, and re-layouts, shards(): jnp.zeros(residual.shape, jnp.float32).at[tree_order]  30.6 us
    psum x1, blocking collectives, shards(): norm_new = lax.psum(jnp.sum(new_residual * new_residual), 'leaf')  30.4 us
    gather x1, local copies, waits for them, and re-layouts, shards(): points[:, tree_order].reshape(dims, leaves_here, LEAF)  29.9 us
  transfers between devices with their start and end apart: 6, of which 3 were waited for; matrix products, arithmetic and copies ran while one was open for 21% of the time, Pallas kernels for 0%

commit v1 on v0

v1 whole, which is shorter than its diff:
```python
import functools
import math

import jax
import jax.numpy as jnp
from jax import lax
from jax.experimental import pallas as pl
from jax.experimental.pallas import tpu as pltpu
from jax.sharding import PartitionSpec as P

LEAF = 256
LEAVES_DEV = 32
REACH = 16
DIM = 32
NODES = 62
WAYS = 4

epsilon = 1e-06
half_root = 0.5**0.5
LOG2E = math.log2(math.e)
F32 = jnp.float32
BF16 = jnp.bfloat16
VMEM = pl.BlockSpec(memory_space=pltpu.VMEM)
SMEM = pl.BlockSpec(memory_space=pltpu.SMEM)


def split(value, count):
    parts = []
    for _ in range(count):
        part = value.astype(BF16).astype(F32)
        parts.append(part)
        value = value - part
    return parts


def norm_row(pts, rate):
    return jnp.sum(pts * pts, axis=0, keepdims=True) * (-rate * LOG2E)


def row_stack(pts, norm):
    high, low = split(pts, 2)
    one = jnp.ones_like(norm)
    width = pts.shape[1]
    tail = jnp.concatenate(split(norm, 3) + [one] * 3 + [jnp.zeros((26, width), F32)], axis=0)
    return jnp.concatenate([high, high, low, tail], axis=0)


def col_stack(pts, norm, rate):
    high, low = split(pts * (2.0 * LOG2E * rate), 2)
    one = jnp.ones_like(norm)
    width = pts.shape[1]
    tail = jnp.concatenate([one] * 3 + split(norm, 3) + [jnp.zeros((26, width), F32)], axis=0)
    return jnp.concatenate([high, low, high, tail], axis=0).astype(BF16)


def tile(rows, cols):
    return jnp.exp2(jnp.dot(rows, cols, preferred_element_type=F32))


def split_rows(row):
    return jnp.concatenate(
        split(row, 3) + [jnp.zeros((13, row.shape[1]), F32)], axis=0
    ).astype(BF16)


LEVELS = []
_first, _width = 0, LEAVES_DEV
while _width >= 2:
    LEVELS.append((_first, _width))
    _first, _width = _first + _width, _width // 2


def up_kernel(perm, rate_ref, pts, dirs, skel, trans, gt, rows_out, ups, raw, held):
    rate = rate_ref[0]
    blocks = pts.shape[1] // 128

    def place(block, _):
        at = pl.multiple_of(block * 128, 128)
        part = pts[:, pl.ds(at, 128)]
        stacked = jnp.concatenate(
            [part, dirs[pl.ds(block, 1), :], norm_row(part, rate), jnp.zeros((94, 128), F32)],
            axis=0,
        )
        raw[pl.ds(at, 128), :] = stacked.T
        return 0

    lax.fori_loop(0, blocks, place, 0, unroll=2)

    def gather(group, _):
        base = pl.multiple_of(group * 32, 32)
        for i in range(32):
            held[pl.ds(base + i, 1), :] = raw[pl.ds(perm[base + i], 1), :]
        return 0

    lax.fori_loop(0, pts.shape[1] // 32, gather, 0)

    def leaf(j, _):
        at = pl.multiple_of(j * LEAF, LEAF)
        mine = held[pl.ds(at, LEAF), :]
        turned = mine.T
        gt[:, pl.ds(at, LEAF)] = turned[:40]
        rows = row_stack(turned[:32], turned[33:34]).T.astype(BF16)
        rows_out[j] = rows
        node = skel[j]
        kern = tile(rows, col_stack(node, norm_row(node, rate), rate))
        ups[pl.ds(j, 1), :] = jnp.sum(kern * mine[:, 32:33], axis=0, keepdims=True)
        return 0

    lax.fori_loop(0, LEAVES_DEV, leaf, 0, unroll=2)

    for first, width in LEVELS:
        for i in range(width // 2):
            total = jnp.zeros((16, LEAF), F32)
            for node in (first + 2 * i, first + 2 * i + 1):
                total = total + jnp.dot(
                    split_rows(ups[node : node + 1, :]), trans[node], preferred_element_type=F32
                )
            ups[first + width + i : first + width + i + 1, :] = (
                jnp.sum(total, axis=0, keepdims=True) * half_root
            )
    ups[63:64, :] = jnp.zeros((1, LEAF), F32)


def down_kernel(
    tgt, src, cnt, first_ref, rate_ref, ridge_ref, perm, gt, left, right, rows, ups, root,
    skel, trans, image, cols, dirs, acc, couple, turned_img,
):
    rate = rate_ref[0]
    first = first_ref[0]

    def load_cols(ref, base):
        def body(i, _):
            at = pl.multiple_of(i * LEAF, LEAF)
            cols[base + i] = col_stack(ref[0:32, pl.ds(at, LEAF)], ref[33:34, pl.ds(at, LEAF)], rate)
            dirs[base + i] = jnp.broadcast_to(ref[32:33, pl.ds(at, LEAF)], (8, LEAF))
            return 0

        lax.fori_loop(0, ref.shape[1] // LEAF, body, 0, unroll=2)

    load_cols(left, 0)
    load_cols(gt, REACH)
    load_cols(right, REACH + LEAVES_DEV)

    lane = lax.broadcasted_iota(jnp.int32, (LEAF, 128), 1)
    couple[...] = jnp.zeros_like(couple)

    def pair(i, _):
        for a, b in ((2 * i, 2 * i + 1), (2 * i + 1, 2 * i)):
            mine, other = skel[a], skel[b]
            kern = tile(
                row_stack(mine, norm_row(mine, rate)).T.astype(BF16),
                col_stack(other, norm_row(other, rate), rate),
            )
            value = jnp.sum(kern * ups[pl.ds(b, 1), :], axis=1, keepdims=True)
            couple[...] = jnp.where(lane == a, value, couple[...])
        return 0

    lax.fori_loop(0, NODES // 2, pair, 0)
    coupled = couple[...].T

    down = {NODES: root[...]}
    for level in range(len(LEVELS) - 1, -1, -1):
        start, width = LEVELS[level]
        for i in range(width // 2):
            parts = split_rows(down[start + width + i])
            for node in (start + 2 * i, start + 2 * i + 1):
                moved = lax.dot_general(
                    parts, trans[node], (((1,), (1,)), ((), ())), preferred_element_type=F32
                )
                down[node] = coupled[node : node + 1] + jnp.sum(moved, axis=0, keepdims=True)
    couple[0:LEAVES_DEV, :] = jnp.concatenate(
        [down[j][:, 0:128] for j in range(LEAVES_DEV)], axis=0
    )
    couple[LEAVES_DEV : 2 * LEAVES_DEV, :] = jnp.concatenate(
        [down[j][:, 128:256] for j in range(LEAVES_DEV)], axis=0
    )

    def far(j, _):
        node = skel[j]
        kern = tile(rows[j], col_stack(node, norm_row(node, rate), rate))
        acc[0, j] = (
            kern[:, 0:128] * couple[pl.ds(j, 1), :]
            + kern[:, 128:256] * couple[pl.ds(j + LEAVES_DEV, 1), :]
        )
        for way in range(1, WAYS):
            acc[way, j] = jnp.zeros((LEAF, 128), F32)
        return 0

    lax.fori_loop(0, LEAVES_DEV, far, 0, unroll=2)

    total = cnt[0]

    def near(step, _):
        for way in range(WAYS):
            slot = step * WAYS + way
            target = jnp.clip(tgt[slot] - first, 0, LEAVES_DEV - 1)
            source = jnp.clip(src[slot] - first + REACH, 0, LEAVES_DEV + 2 * REACH - 1)
            weight = jnp.where(slot < total, dirs[source][0:1, :], 0.0)
            kern = tile(rows[target], cols[source]) * weight
            acc[way, target] += kern[:, 0:128] + kern[:, 128:256]
        return 0

    lax.fori_loop(0, (total + WAYS - 1) // WAYS, near, 0)

    turned_img[...] = jnp.zeros_like(turned_img)

    def gather_image(j, _):
        value = acc[0, j]
        for way in range(1, WAYS):
            value = value + acc[way, j]
        turned_img[...] = jnp.where(
            lane == j, jnp.sum(value, axis=1, keepdims=True), turned_img[...]
        )
        return 0

    lax.fori_loop(0, LEAVES_DEV, gather_image, 0)
    tree_image = turned_img[...].T

    grand = jnp.zeros((192, 128), F32)
    high_id = lax.broadcasted_iota(jnp.int32, (64, LEAF), 0)
    low_id = lax.broadcasted_iota(jnp.int32, (128, LEAF), 0)
    for j in range(LEAVES_DEV):
        at = perm[j : j + 1, :]
        value = tree_image[j : j + 1, :] + ridge_ref[0] * dirs[REACH + j][0:1, :]
        hot = high_id == (at >> 7)
        picked = jnp.concatenate(
            [jnp.where(hot, part, 0.0) for part in split(value, 3)], axis=0
        ).astype(BF16)
        low = jnp.where(low_id == (at & 127), 1.0, 0.0).astype(BF16)
        grand = grand + lax.dot_general(
            picked, low, (((1,), (1,)), ((), ())), preferred_element_type=F32
        )
    image[...] = grand[0:64] + grand[64:128] + grand[128:192]


PARAMS = pltpu.CompilerParams(vmem_limit_bytes=60 * 1024 * 1024)


def call_up(perm, rate, points, direction, skeleton, transfer):
    count = points.shape[1]
    return pl.pallas_call(
        up_kernel,
        out_shape=(
            jax.ShapeDtypeStruct((40, count), F32),
            jax.ShapeDtypeStruct((LEAVES_DEV, LEAF, 128), BF16),
            jax.ShapeDtypeStruct((64, LEAF), F32),
        ),
        in_specs=[SMEM, SMEM, VMEM, VMEM, VMEM, VMEM],
        out_specs=(VMEM, VMEM, VMEM),
        scratch_shapes=[pltpu.VMEM((count, 128), F32), pltpu.VMEM((count, 128), F32)],
        compiler_params=PARAMS,
        name="up_tree",
    )(perm, rate, points, direction, skeleton, transfer)


def call_down(tgt, src, cnt, first, rate, ridge, perm, gt, left, right, rows, ups, root, skel, trans):
    return pl.pallas_call(
        down_kernel,
        out_shape=jax.ShapeDtypeStruct((64, 128), F32),
        in_specs=[SMEM] * 6 + [VMEM] * 9,
        out_specs=VMEM,
        scratch_shapes=[
            pltpu.VMEM((LEAVES_DEV + 2 * REACH, 128, LEAF), BF16),
            pltpu.VMEM((LEAVES_DEV + 2 * REACH, 8, LEAF), F32),
            pltpu.VMEM((WAYS, LEAVES_DEV, LEAF, 128), F32),
            pltpu.VMEM((LEAF, 128), F32),
            pltpu.VMEM((LEAF, 128), F32),
        ],
        compiler_params=PARAMS,
        name="down_near",
    )(tgt, src, cnt, first, rate, ridge, perm, gt, left, right, rows, ups, root, skel, trans)


def partner(value, axis, distance):
    mask = 2**distance
    pairs = [(source, source ^ mask) for source in range(lax.axis_size(axis))]
    return lax.ppermute(value, axis, pairs)


def kernel_block(first_set, second_set, rate_value):
    first_norms = jnp.sum(first_set * first_set, axis=-2)
    second_norms = jnp.sum(second_set * second_set, axis=-2)
    inner_prod = jnp.einsum(
        "...dm,...dn->...mn", first_set, second_set, precision=lax.Precision.HIGHEST
    )
    distance = first_norms[..., :, None] + second_norms[..., None, :] - 2.0 * inner_prod
    return jnp.exp(-rate_value * distance)


def shards(
    points,
    solution,
    residual,
    direction,
    ridge_weight,
    kernel_rate,
    tree_perm,
    local_skeleton,
    local_transfer,
    cross_skeleton,
    cross_transfer,
    near_target,
    near_source,
    tile_count,
):
    rate_value = kernel_rate[0]
    devices = lax.axis_size("leaf")
    device_index = lax.axis_index("leaf")
    gt, rows, ups = call_up(
        tree_perm[0], kernel_rate, points, direction.reshape(64, 128), local_skeleton, local_transfer
    )
    edge = REACH * LEAF
    onward = [(i, (i + 1) % devices) for i in range(devices - 1)]
    back = [(j, i) for i, j in onward]
    left = lax.ppermute(gt[:, gt.shape[1] - edge :], "leaf", onward)
    right = lax.ppermute(gt[:, :edge], "leaf", back)
    levels = devices.bit_length() - 1
    couple_kernel = kernel_block(cross_skeleton[:, 0], cross_skeleton[:, 1], rate_value)
    own_transfer = cross_transfer[:, 0].astype(jnp.float32)
    current = ups[NODES]
    sibling_list = []
    for level in range(levels):
        sibling_value = partner(current, "leaf", level)
        sibling_list.append(sibling_value)
        if level < levels - 1:
            mine_lift = jnp.dot(current, own_transfer[level], precision=lax.Precision.HIGHEST)
            other_lift = jnp.dot(
                sibling_value,
                cross_transfer[level, 1].astype(jnp.float32),
                precision=lax.Precision.HIGHEST,
            )
            current = (mine_lift + other_lift) * half_root
    sibling_values = jnp.stack(sibling_list)
    cross_values = jnp.einsum(
        "lrs,ls->lr", couple_kernel, sibling_values, precision=lax.Precision.HIGHEST
    )
    current = cross_values[levels - 1]
    for level in range(levels - 2, -1, -1):
        current = cross_values[level] + jnp.dot(
            own_transfer[level], current, precision=lax.Precision.HIGHEST
        )
    own_first = (device_index * LEAVES_DEV).astype(jnp.int32).reshape(1)
    image = call_down(
        near_target, near_source, tile_count, own_first, kernel_rate, ridge_weight,
        tree_perm.reshape(LEAVES_DEV, LEAF), gt, left, right, rows, ups, current.reshape(1, LEAF),
        local_skeleton, local_transfer,
    ).reshape(-1)
    norm_old, curvature = lax.psum(
        (jnp.sum(residual * residual), jnp.sum(direction * image)), "leaf"
    )
    step_size = norm_old / curvature
    new_residual = residual - step_size * image
    norm_new = lax.psum(jnp.sum(new_residual * new_residual), "leaf")
    new_solution = solution + step_size * direction
    new_direction = new_residual + norm_new / (norm_old + epsilon) * direction
    return (new_solution, new_residual, new_direction)


def solution(mesh):
    return jax.shard_map(
        shards,
        mesh=mesh,
        in_specs=(
            P(None, ("groups", "leaf")),
            P(("groups", "leaf")),
            P(("groups", "leaf")),
            P(("groups", "leaf")),
            P("groups"),
            P("groups"),
            P(("groups", "leaf"), None),
            P(("groups", "leaf"), None, None),
            P(("groups", "leaf"), None, None),
            P(("groups", "leaf"), None, None, None),
            P(("groups", "leaf"), None, None, None),
            P(("groups", "leaf")),
            P(("groups", "leaf")),
            P(("groups", "leaf")),
        ),
        out_specs=(P(("groups", "leaf")), P(("groups", "leaf")), P(("groups", "leaf"))),
        check_vma=False,
    )
```

time: 617 us -> 178 us (0.29); the launches traced: 610 us -> 180 us
  local copies, waits for them, and re-layouts: 189 us -> 5.46 us
  matrix products: 165 us -> 4.32 us
  blocking collectives: 197 us -> 72.2 us
  Pallas kernels: 0 us -> 61.6 us
  other arithmetic: 33.1 us -> 5.64 us
    gather x34 -> x0, local copies, waits for them, and re-layouts: 127 us -> none  [the longest x1 45.5 us: shards(): tree_dir = direction[tree_order].reshape(leaves_here, LEAF)]
    psum x1, blocking collectives: 167 us -> 42.1 us  [shards(): lax.psum((jnp.sum(residual * residual), jnp.sum(direction * image)), 'leaf')]
    dot_general x49 -> x0, matrix products: 97.7 us -> none  [the longest x16 36.9 us: tile_block(): jnp.einsum('bij,bj->bi', block_kernel, source_pack[:, dims], precision=la...]
    pallas_call x0 -> x2, Pallas kernels: none -> 61.6 us  [the longest x1 37.1 us: call_down(): pl.pallas_call(down_kernel, out_shape=jax.ShapeDtypeStruct((64, 128), F32...]
    dot_general x23 -> x1, matrix products: 62.7 us -> 1.17 us  [kernel_block(): jnp.einsum('...dm,...dn->...mn', first_set, second_set, precision=lax.Pre...]
    scatter x1 -> x0, local copies, waits for them, and re-layouts: 30.6 us -> none  [shards(): jnp.zeros(residual.shape, jnp.float32).at[tree_order]]
    convert_element_type x16 -> x0, other arithmetic: 10.4 us -> none  [tile_block(): alive_mask = (slot_ids < tile_total).astype(jnp.float32)]
    reshape x14 -> x1, local copies, waits for them, and re-layouts: 8.98 us -> 0.62 us  [shards(): tree_perm.reshape(LEAVES_DEV, LEAF)]
  transfers between devices with their start and end apart: 6 -> 6, of which waited for: 3 -> 2; matrix products, arithmetic and copies ran while one was open for 21% -> 6% of each run, Pallas kernels for 0% -> 0%
where the time goes in v1:
time: 178 us; the launch traced here: 180 us
  blocking collectives  72.2 us (41%)
  Pallas kernels  61.6 us (35%)
  starting transfers between devices  17.5 us (10%)
  waiting for transfers between devices  7.73 us (4%)
  other arithmetic  5.64 us (3%)
  local copies, waits for them, and re-layouts  5.46 us (3%)
  between operations  5.34 us (3%)
  matrix products  4.32 us (2%)
    psum x1, blocking collectives, shards(): lax.psum((jnp.sum(residual * residual), jnp.sum(direction * image)), 'leaf')  42.1 us
    pallas_call x1, Pallas kernels, call_down(): pl.pallas_call(down_kernel, out_shape=jax.ShapeDtypeStruct((64, 128), F32...  37.1 us
    psum x1, blocking collectives, shards(): norm_new = lax.psum(jnp.sum(new_residual * new_residual), 'leaf')  30.1 us
    pallas_call x1, Pallas kernels, call_up(): pl.pallas_call(up_kernel, out_shape=(jax.ShapeDtypeStruct((40, count), F3...  24.5 us
    ppermute x4, starting transfers between devices, partner(): return lax.ppermute(value, axis, pairs)  14.2 us
    ppermute x4, waiting for transfers between devices, partner(): return lax.ppermute(value, axis, pairs)  7.73 us
  transfers between devices with their start and end apart: 6, of which 2 were waited for; matrix products, arithmetic and copies ran while one was open for 6% of the time, Pallas kernels for 0%

profile of v1, /device:TPU:0, one launch (start us, length us, event | category | flops | bytes accessed | tf_op | source)
XLA Modules:
  0.0 179.8 jit_solution(15561544923501506718)
XLA Ops:
  1.3 24.5 %up_tree.1 = (f32[40,8192]{1,0:T(8,128)}, bf16[32,256,128]{2,1,0:T(8,128)(2,1)}, f32[64,256]{1,0:T(8,128)}) custom-call(s32[8192]{0:T(1024)} %bitcast.94, f32[1]{0:T(128)S(6)} %copy.24.rate_ref, f32[32,8192]{1,0:T(8,128)} %pts.1, f32[64,128]{1,0:T(8,128)} %bitcast.93, f32[62,32,256]{2,1,0:T(8,128)} %skel.3, bf16[62,256,256]{2,1,0:T(8,128)(2,1)} %trans.3), custom_call_target="tpu_custom_call" | custom-call | tf_op jit(solution)/shard_map/up_tree/pallas_call | solution.py:241
  25.8 0.7 slice.59
  27.0 2.5 %fusion.43 = (f32[40,4096]{1,0:T(8,128)}, f32[40,4096]{1,0:T(8,128)}) fusion(f32[40,8192]{1,0:T(8,128)} %get-tuple-element.6.gt), kind=kLoop, calls=%fused_computation.57 | loop fusion | bytes 2621440 | tf_op jit(solution)/shard_map/slice | solution.py:316
  29.5 2.0 %collective-permute-start = (f32[40,4096]{1,0:T(8,128)}, f32[40,4096]{1,0:T(8,128)S(1)}, u32[]{:S(2)}, u32[]{:S(2)}) collective-permute-start(f32[40,4096]{1,0:T(8,128)} %get-tuple-element.16), channel_id=1, source_target_pairs={{0,1},{1,2},{2,3},{3,4},{4,5},{5,6},{6,7},{7,8},{8,9},{9,10},{10,1... | collective-permute-start | bytes 1966088 | tf_op jit(solution)/shard_map/ppermute | solution.py:315
  31.5 1.3 collective-permute-start.1
  32.9 1.2 fusion.2
  34.1 0.8 fusion.19
  35.1 4.8 %collective-permute-start.3 = (f32[256]{0:T(256)S(1)}, f32[256]{0:T(256)S(1)}, u32[]{:S(2)}, u32[]{:S(2)}) collective-permute-start(f32[256]{0:T(256)S(1)} %add_multiply_fusion.2), channel_id=1, source_target_pairs={{0,2},{1,3},{2,0},{3,1},{4,6},{5,7},{6,4},{7,5},{8,10},{9,11},{10,... | collective-permute-start | bytes 3080 | tf_op jit(solution)/shard_map/ppermute | solution.py:277
  40.1 6.3 %collective-permute-done.3 = f32[256]{0:T(256)S(1)} collective-permute-done((f32[256]{0:T(256)S(1)}, f32[256]{0:T(256)S(1)}, u32[]{:S(2)}, u32[]{:S(2)}) %collective-permute-start.3) | collective-permute-done | bytes 1056 | tf_op jit(solution)/shard_map/ppermute | solution.py:277
  46.5 5.8 %collective-permute-start.4 = (f32[256]{0:T(256)S(1)}, f32[256]{0:T(256)S(1)}, u32[]{:S(2)}, u32[]{:S(2)}) collective-permute-start(f32[256]{0:T(256)S(1)} %add_multiply_fusion.1), channel_id=1, source_target_pairs={{0,4},{1,5},{2,6},{3,7},{4,0},{5,1},{6,2},{7,3},{8,12},{9,13},{10,... | collective-permute-start | bytes 3080 | tf_op jit(solution)/shard_map/ppermute | solution.py:277
  52.5 1.4 collective-permute-done.4
  54.0 3.1 %collective-permute-start.5 = (f32[256]{0:T(256)S(1)}, f32[256]{0:T(256)S(1)}, u32[]{:S(2)}, u32[]{:S(2)}) collective-permute-start(f32[256]{0:T(256)S(1)} %add_multiply_fusion), channel_id=1, source_target_pairs={{0,8},{1,9},{2,10},{3,11},{4,12},{5,13},{6,14},{7,15},{8,0},{9,1},... | collective-permute-start | bytes 3080 | tf_op jit(solution)/shard_map/ppermute | solution.py:277
  57.1 0.7 multiply_reduce_fusion.1
  58.3 0.7 reduce.3
  59.0 0.6 reshape.31.perm
  61.0 1.0 fusion.38
  62.7 0.6 add.54
  63.4 0.8 copy-done.1
  64.4 37.1 %down_near.1 = f32[64,128]{1,0:T(8,128)} custom-call(s32[256]{0:T(256)} %tgt.1, s32[256]{0:T(256)} %src.1, s32[1]{0:T(128)S(6)} %copy.25.cnt, s32[1]{0:T(128)} %bitcast.first_ref, f32[1]{0:T(128)S(6)} %copy.24.rate_ref, f32[1]{0:T(128)S(6)} %copy.23.ridge_ref, s32[32,256]{1,0:T(8,128)} %reshape.31.perm, f32[40,8192]{1,0:T(8,128)} %get-tuple-element.6.gt, ...), custom_call_target="tpu_custom_call" | custom-call | tf_op jit(solution)/shard_map/down_near/pallas_call | solution.py:257
  101.5 1.4 fusion.36
  102.9 42.1 %all-reduce = (f32[]{:T(128)}, f32[]{:T(128)}) all-reduce(f32[]{:T(128)} %multiply_reduce_fusion.1, f32[]{:T(128)} %fusion.36), channel_id=1, replica_groups=mesh['groups'=2,'leaf'=16] {'leaf'}, use_global_device_ids=true, to_apply=%region_1.0 | all-reduce | flops 2 | bytes 16 | tf_op jit(solution)/shard_map/psum | solution.py:348
  146.3 1.5 multiply_reduce_fusion
  147.8 30.1 %psum.23 = f32[]{:T(128)} all-reduce(f32[]{:T(128)} %get-tuple-element.13), channel_id=1, replica_groups=mesh['groups'=2,'leaf'=16] {'leaf'}, use_global_device_ids=true, to_apply=%region_7.0 | all-reduce | flops 1 | bytes 8 | tf_op jit(solution)/shard_map/psum | solution.py:353
  179.2 0.6 multiply_add_fusion
  (40 shorter events, 2.7 us)
Async XLA Ops:
  25.8 7.0 %copy-start.4 = (f32[4,2,32,256]{3,2,1,0:T(8,128)S(1)}, f32[4,2,32,256]{3,2,1,0:T(8,128)}, u32[]{:S(2)}) copy-start(f32[4,2,32,256]{3,2,1,0:T(8,128)} %param.23) | copy-start | bytes 786436
  26.6 8.3 %collective-permute-start.2 = (f32[256]{0:T(256)S(1)}, f32[256]{0:T(256)S(1)}, u32[]{:S(2)}, u32[]{:S(2)}) collective-permute-start(f32[256]{0:T(256)S(1)} %bitcast.120), channel_id=1, source_target_pairs={{0,1},{1,0},{2,3},{3,2},{4,5},{5,4},{6,7},{7,6},{8,9},{9,8},{10,11... | collective-permute-start | bytes 3080 | tf_op jit(solution)/shard_map/ppermute | solution.py:277
  27.0 7.0 %copy-start = (bf16[3,2,256,256]{3,2,1,0:T(8,128)(2,1)S(1)}, bf16[3,2,256,256]{3,2,1,0:T(8,128)(2,1)}, u32[]{:S(2)}) copy-start(bf16[3,2,256,256]{3,2,1,0:T(8,128)(2,1)} %param.24) | copy-start | bytes 2359300
  27.0 30.1 %copy-start.7 = (f32[8192]{0:T(1024)S(1)}, f32[8192]{0:T(1024)}, u32[]{:S(2)}) copy-start(f32[8192]{0:T(1024)} %param.16) | copy-start | bytes 98308
  27.0 31.3 %copy-start.5 = (s32[1,8192]{1,0:T(1,128)S(1)}, s32[1,8192]{1,0:T(1,128)}, u32[]{:S(2)}) copy-start(s32[1,8192]{1,0:T(1,128)} %param.20) | copy-start | bytes 98308
  29.5 33.8 %collective-permute-start = (f32[40,4096]{1,0:T(8,128)}, f32[40,4096]{1,0:T(8,128)S(1)}, u32[]{:S(2)}, u32[]{:S(2)}) collective-permute-start(f32[40,4096]{1,0:T(8,128)} %get-tuple-element.16), channel_id=1, source_target_pairs={{0,1},{1,2},{2,3},{3,4},{4,5},{5,6},{6,7},{7,8},{8,9},{9,10},{10,1... | collective-permute-start | bytes 1966088 | tf_op jit(solution)/shard_map/ppermute | solution.py:315
  31.5 31.8 %collective-permute-start.1 = (f32[40,4096]{1,0:T(8,128)}, f32[40,4096]{1,0:T(8,128)S(1)}, u32[]{:S(2)}, u32[]{:S(2)}) collective-permute-start(f32[40,4096]{1,0:T(8,128)} %get-tuple-element.15), channel_id=1, source_target_pairs={{1,0},{2,1},{3,2},{4,3},{5,4},{6,5},{7,6},{8,7},{9,8},{10,9},{11,1... | collective-permute-start | bytes 1966088 | tf_op jit(solution)/shard_map/ppermute | solution.py:316
  35.1 11.3 %collective-permute-start.3 = (f32[256]{0:T(256)S(1)}, f32[256]{0:T(256)S(1)}, u32[]{:S(2)}, u32[]{:S(2)}) collective-permute-start(f32[256]{0:T(256)S(1)} %add_multiply_fusion.2), channel_id=1, source_target_pairs={{0,2},{1,3},{2,0},{3,1},{4,6},{5,7},{6,4},{7,5},{8,10},{9,11},{10,... | collective-permute-start | bytes 3080 | tf_op jit(solution)/shard_map/ppermute | solution.py:277
  46.5 7.4 %collective-permute-start.4 = (f32[256]{0:T(256)S(1)}, f32[256]{0:T(256)S(1)}, u32[]{:S(2)}, u32[]{:S(2)}) collective-permute-start(f32[256]{0:T(256)S(1)} %add_multiply_fusion.1), channel_id=1, source_target_pairs={{0,4},{1,5},{2,6},{3,7},{4,0},{5,1},{6,2},{7,3},{8,12},{9,13},{10,... | collective-permute-start | bytes 3080 | tf_op jit(solution)/shard_map/ppermute | solution.py:277
  54.0 6.9 %collective-permute-start.5 = (f32[256]{0:T(256)S(1)}, f32[256]{0:T(256)S(1)}, u32[]{:S(2)}, u32[]{:S(2)}) collective-permute-start(f32[256]{0:T(256)S(1)} %add_multiply_fusion), channel_id=1, source_target_pairs={{0,8},{1,9},{2,10},{3,11},{4,12},{5,13},{6,14},{7,15},{8,0},{9,1},... | collective-permute-start | bytes 3080 | tf_op jit(solution)/shard_map/ppermute | solution.py:277
  63.3 0.8 copy-start.1
  63.3 1.0 copy-start.2
  64.4 37.1 %copy-start.3 = (f32[8192]{0:T(1024)S(1)}, f32[8192]{0:T(1024)}, u32[]{:S(2)}) copy-start(f32[8192]{0:T(1024)} %param.17) | copy-start | bytes 98308
  64.4 114.8 %copy-start.8 = (f32[8192]{0:T(1024)S(1)}, f32[8192]{0:T(1024)}, u32[]{:S(2)}) copy-start(f32[8192]{0:T(1024)} %param.15) | copy-start | bytes 98308
  147.8 32.1 %copy-start.6 = (f32[8192]{0:T(1024)}, f32[8192]{0:T(1024)S(1)}, u32[]{:S(2)}) copy-start(f32[8192]{0:T(1024)S(1)} %get-tuple-element.14) | copy-start | bytes 98308

commit v2 on v1

--- a/solution.py
+++ b/solution.py
@@ -195,6 +195,7 @@
             slot = step * WAYS + way
             target = jnp.clip(tgt[slot] - first, 0, LEAVES_DEV - 1)
             source = jnp.clip(src[slot] - first + REACH, 0, LEAVES_DEV + 2 * REACH - 1)
+            source = jnp.where(slot < total, source, target + REACH)
             weight = jnp.where(slot < total, dirs[source][0:1, :], 0.0)
             kern = tile(rows[target], cols[source]) * weight
             acc[way, target] += kern[:, 0:128] + kern[:, 128:256]
@@ -271,20 +272,223 @@
     )(tgt, src, cnt, first, rate, ridge, perm, gt, left, right, rows, ups, root, skel, trans)
 
 
-def partner(value, axis, distance):
-    mask = 2**distance
-    pairs = [(source, source ^ mask) for source in range(lax.axis_size(axis))]
-    return lax.ppermute(value, axis, pairs)
-
-
-def kernel_block(first_set, second_set, rate_value):
-    first_norms = jnp.sum(first_set * first_set, axis=-2)
-    second_norms = jnp.sum(second_set * second_set, axis=-2)
-    inner_prod = jnp.einsum(
-        "...dm,...dn->...mn", first_set, second_set, precision=lax.Precision.HIGHEST
-    )
-    distance = first_norms[..., :, None] + second_norms[..., None, :] - 2.0 * inner_prod
-    return jnp.exp(-rate_value * distance)
+def remote_params(collective_id):
+    return pltpu.CompilerParams(
+        vmem_limit_bytes=60 * 1024 * 1024, collective_id=collective_id, has_side_effects=True
+    )
+
+
+def signal(barrier, device):
+    pl.semaphore_signal(
+        barrier, inc=1, device_id={"leaf": device}, device_id_type=pl.DeviceIdType.MESH
+    )
+
+
+def remote(src, dst, send_sem, recv_sem, device):
+    return pltpu.make_async_remote_copy(
+        src_ref=src,
+        dst_ref=dst,
+        send_sem=send_sem,
+        recv_sem=recv_sem,
+        device_id={"leaf": device},
+        device_id_type=pl.DeviceIdType.MESH,
+    )
+
+
+def cross_kernel(
+    devices, rate_ref, ups, skel, trans, gt, down, left, right,
+    sent, slots, kerns, couple, halo_send, halo_recv, hop_send, hop_recv,
+):
+    rate = rate_ref[0]
+    me = lax.axis_index("leaf")
+    levels = skel.shape[0]
+    edge = left.shape[1]
+    peers = []
+    for level in range(levels):
+        mask = 2**level
+        peers.append(me + mask * (1 - 2 * ((me // mask) % 2)))
+    has_left, has_right = me > 0, me < devices - 1
+
+    barrier = pltpu.get_barrier_semaphore()
+    for peer in peers:
+        signal(barrier, peer)
+    for present, peer in ((has_left, me - 1), (has_right, me + 1)):
+
+        @pl.when(present)
+        def _():
+            signal(barrier, peer)
+
+    pl.semaphore_wait(
+        barrier, levels + has_left.astype(jnp.int32) + has_right.astype(jnp.int32)
+    )
+
+    def hop(level):
+        return remote(
+            sent.at[level], slots.at[level], hop_send.at[level], hop_recv.at[level], peers[level]
+        )
+
+    to_left = remote(
+        gt.at[:, pl.ds(0, edge)], right, halo_send.at[0], halo_recv.at[0], me - 1
+    )
+    to_right = remote(
+        gt.at[:, pl.ds(gt.shape[1] - edge, edge)], left, halo_send.at[1], halo_recv.at[1], me + 1
+    )
+
+    current = ups[NODES : NODES + 1, :]
+    sent[0] = jnp.broadcast_to(current, (8, LEAF))
+    hop(0).start()
+    pl.when(has_left)(to_left.start)
+    pl.when(has_right)(to_right.start)
+
+    def couplings(level, _):
+        mine, other = skel[level, 0], skel[level, 1]
+        kerns[level] = tile(
+            row_stack(mine, norm_row(mine, rate)).T.astype(BF16),
+            col_stack(other, norm_row(other, rate), rate),
+        )
+        return 0
+
+    lax.fori_loop(0, levels, couplings, 0)
+    for level in range(levels):
+        hop(level).wait()
+        if level < levels - 1:
+            total = jnp.dot(
+                split_rows(current), trans[level, 0], preferred_element_type=F32
+            ) + jnp.dot(
+                split_rows(slots[level][0:1]), trans[level, 1], preferred_element_type=F32
+            )
+            current = jnp.sum(total, axis=0, keepdims=True) * half_root
+            sent[level + 1] = jnp.broadcast_to(current, (8, LEAF))
+            hop(level + 1).start()
+    lane = lax.broadcasted_iota(jnp.int32, (LEAF, 128), 1)
+    picked = jnp.zeros((LEAF, 128), F32)
+    for level in range(levels):
+        value = jnp.sum(kerns[level] * slots[level][0:1], axis=1, keepdims=True)
+        picked = jnp.where(lane == level, value, picked)
+    couple[...] = picked.T
+    current = couple[levels - 1 : levels, :]
+    for level in range(levels - 2, -1, -1):
+        moved = lax.dot_general(
+            split_rows(current), trans[level, 0], (((1,), (1,)), ((), ())),
+            preferred_element_type=F32,
+        )
+        current = couple[level : level + 1, :] + jnp.sum(moved, axis=0, keepdims=True)
+    down[...] = current
+
+    @pl.when(has_left)
+    def _():
+        to_left.wait_send()
+        to_right.wait_recv()
+
+    @pl.when(has_right)
+    def _():
+        to_right.wait_send()
+        to_left.wait_recv()
+
+
+def call_cross(devices, rate, ups, skel, trans, gt):
+    levels = skel.shape[0]
+    edge = REACH * LEAF
+    return pl.pallas_call(
+        functools.partial(cross_kernel, devices),
+        out_shape=(
+            jax.ShapeDtypeStruct((1, LEAF), F32),
+            jax.ShapeDtypeStruct((40, edge), F32),
+            jax.ShapeDtypeStruct((40, edge), F32),
+        ),
+        in_specs=[SMEM, VMEM, VMEM, VMEM, pl.BlockSpec(memory_space=pl.ANY)],
+        out_specs=(
+            VMEM, pl.BlockSpec(memory_space=pl.ANY), pl.BlockSpec(memory_space=pl.ANY),
+        ),
+        scratch_shapes=[
+            pltpu.VMEM((levels, 8, LEAF), F32),
+            pltpu.VMEM((levels, 8, LEAF), F32),
+            pltpu.VMEM((levels, LEAF, LEAF), F32),
+            pltpu.VMEM((128, LEAF), F32),
+            pltpu.SemaphoreType.DMA((2,)),
+            pltpu.SemaphoreType.DMA((2,)),
+            pltpu.SemaphoreType.DMA((levels,)),
+            pltpu.SemaphoreType.DMA((levels,)),
+        ],
+        compiler_params=remote_params(0),
+        name="cross_levels",
+    )(rate, ups, skel, trans, gt)
+
+
+def step_kernel(
+    devices, image, solution, residual, direction, new_solution, new_residual, new_direction,
+    sent, slots, send_sem, recv_sem,
+):
+    me = lax.axis_index("leaf")
+    barrier = pltpu.get_barrier_semaphore()
+
+    def greet(offset, _):
+        signal(barrier, (me + offset) % devices)
+        return 0
+
+    lax.fori_loop(1, devices, greet, 0)
+    res, dire, img = residual[...], direction[...], image[...]
+    sent[0] = jnp.concatenate(
+        [
+            jnp.sum(res * res, axis=0, keepdims=True),
+            jnp.sum(dire * img, axis=0, keepdims=True),
+            jnp.zeros((6, 128), F32),
+        ],
+        axis=0,
+    )
+    pl.semaphore_wait(barrier, devices - 1)
+
+    def total(phase):
+        def copy(offset):
+            return remote(
+                sent.at[phase],
+                slots.at[phase, offset],
+                send_sem.at[phase, offset],
+                recv_sem.at[phase, offset],
+                (me + offset) % devices,
+            )
+
+        def start(offset, _):
+            copy(offset).start()
+            return 0
+
+        def finish(offset, running):
+            copy(offset).wait()
+            return running + slots[phase, offset]
+
+        lax.fori_loop(1, devices, start, 0)
+        lanes = lax.fori_loop(1, devices, finish, sent[phase])
+        return jnp.sum(lanes, axis=1, keepdims=True)
+
+    sums = total(0)
+    norm_old = sums[0:1]
+    step_size = norm_old / sums[1:2]
+    new_res = res - step_size * img
+    new_residual[...] = new_res
+    sent[1] = jnp.concatenate(
+        [jnp.sum(new_res * new_res, axis=0, keepdims=True), jnp.zeros((7, 128), F32)], axis=0
+    )
+    norm_new = total(1)[0:1]
+    new_solution[...] = solution[...] + step_size * dire
+    new_direction[...] = new_res + norm_new / (norm_old + epsilon) * dire
+
+
+def call_step(devices, image, solution, residual, direction):
+    flat = jax.ShapeDtypeStruct((64, 128), F32)
+    return pl.pallas_call(
+        functools.partial(step_kernel, devices),
+        out_shape=(flat, flat, flat),
+        in_specs=[VMEM] * 4,
+        out_specs=(VMEM,) * 3,
+        scratch_shapes=[
+            pltpu.VMEM((2, 8, 128), F32),
+            pltpu.VMEM((2, devices, 8, 128), F32),
+            pltpu.SemaphoreType.DMA((2, devices)),
+            pltpu.SemaphoreType.DMA((2, devices)),
+        ],
+        compiler_params=remote_params(1),
+        name="step",
+    )(image, solution, residual, direction)
 
 
 def shards(
@@ -303,57 +507,21 @@
     near_source,
     tile_count,
 ):
-    rate_value = kernel_rate[0]
     devices = lax.axis_size("leaf")
-    device_index = lax.axis_index("leaf")
+    folded = tuple(array.reshape(64, 128) for array in (solution, residual, direction))
     gt, rows, ups = call_up(
-        tree_perm[0], kernel_rate, points, direction.reshape(64, 128), local_skeleton, local_transfer
-    )
-    edge = REACH * LEAF
-    onward = [(i, (i + 1) % devices) for i in range(devices - 1)]
-    back = [(j, i) for i, j in onward]
-    left = lax.ppermute(gt[:, gt.shape[1] - edge :], "leaf", onward)
-    right = lax.ppermute(gt[:, :edge], "leaf", back)
-    levels = devices.bit_length() - 1
-    couple_kernel = kernel_block(cross_skeleton[:, 0], cross_skeleton[:, 1], rate_value)
-    own_transfer = cross_transfer[:, 0].astype(jnp.float32)
-    current = ups[NODES]
-    sibling_list = []
-    for level in range(levels):
-        sibling_value = partner(current, "leaf", level)
-        sibling_list.append(sibling_value)
-        if level < levels - 1:
-            mine_lift = jnp.dot(current, own_transfer[level], precision=lax.Precision.HIGHEST)
-            other_lift = jnp.dot(
-                sibling_value,
-                cross_transfer[level, 1].astype(jnp.float32),
-                precision=lax.Precision.HIGHEST,
-            )
-            current = (mine_lift + other_lift) * half_root
-    sibling_values = jnp.stack(sibling_list)
-    cross_values = jnp.einsum(
-        "lrs,ls->lr", couple_kernel, sibling_values, precision=lax.Precision.HIGHEST
-    )
-    current = cross_values[levels - 1]
-    for level in range(levels - 2, -1, -1):
-        current = cross_values[level] + jnp.dot(
-            own_transfer[level], current, precision=lax.Precision.HIGHEST
-        )
-    own_first = (device_index * LEAVES_DEV).astype(jnp.int32).reshape(1)
+        tree_perm[0], kernel_rate, points, folded[2], local_skeleton, local_transfer
+    )
+    root, left, right = call_cross(
+        devices, kernel_rate, ups, cross_skeleton, cross_transfer, gt
+    )
+    own_first = (lax.axis_index("leaf") * LEAVES_DEV).astype(jnp.int32).reshape(1)
     image = call_down(
         near_target, near_source, tile_count, own_first, kernel_rate, ridge_weight,
-        tree_perm.reshape(LEAVES_DEV, LEAF), gt, left, right, rows, ups, current.reshape(1, LEAF),
+        tree_perm.reshape(LEAVES_DEV, LEAF), gt, left, right, rows, ups, root,
         local_skeleton, local_transfer,
-    ).reshape(-1)
-    norm_old, curvature = lax.psum(
-        (jnp.sum(residual * residual), jnp.sum(direction * image)), "leaf"
-    )
-    step_size = norm_old / curvature
-    new_residual = residual - step_size * image
-    norm_new = lax.psum(jnp.sum(new_residual * new_residual), "leaf")
-    new_solution = solution + step_size * direction
-    new_direction = new_residual + norm_new / (norm_old + epsilon) * direction
-    return (new_solution, new_residual, new_direction)
+    )
+    return tuple(array.reshape(-1) for array in call_step(devices, image, *folded))
 
 
 def solution(mesh):

time: 178 us -> 125 us (0.70)
  blocking collectives: 72.2 us -> 0 us
  Pallas kernels: 61.6 us -> 116 us
  starting transfers between devices: 17.5 us -> 0 us
  waiting for transfers between devices: 7.73 us -> 0 us
  matrix products: 4.32 us -> 0 us
  other arithmetic: 5.64 us -> 1.48 us
  between operations: 5.34 us -> 2.59 us
    psum x2 -> x0, blocking collectives: 72.2 us -> none  [the longest x1 42.1 us: shards(): lax.psum((jnp.sum(residual * residual), jnp.sum(direction * image)), 'leaf')]
    pallas_call x0 -> x2, Pallas kernels: none -> 55.4 us  [the longest x1 29.8 us: call_cross(): pl.pallas_call(functools.partial(cross_kernel, devices), out_shape=(jax.S...]
    ppermute x6 -> x0, starting transfers between devices: 17.5 us -> none  [the longest x4 14.2 us: partner(): return lax.ppermute(value, axis, pairs)]
    ppermute x6 -> x0, waiting for transfers between devices: 7.73 us -> none  [the longest x4 7.73 us: partner(): return lax.ppermute(value, axis, pairs)]
    dot_general x11 -> x0, matrix products: 4.32 us -> none  [the longest x1 1.17 us: kernel_block(): jnp.einsum('...dm,...dn->...mn', first_set, second_set, precision=lax.Pre...]
    reduce_sum x4 -> x0, other arithmetic: 3.53 us -> none  [the longest x1 1.45 us: shards(): norm_new = lax.psum(jnp.sum(new_residual * new_residual), 'leaf')]
    slice x3 -> x0, local copies, waits for them, and re-layouts: 3.25 us -> none  [the longest x1 2.5 us: shards(): right = lax.ppermute(gt[:, :edge], 'leaf', back)]
    unnamed x19 -> x4, local copies, waits for them, and re-layouts: 1.58 us -> 4.64 us
  transfers between devices with their start and end apart: 6 -> 0, of which waited for: 2 -> 0; matrix products, arithmetic and copies ran while one was open for 6% -> 0% of each run, Pallas kernels for 0% -> 0%
where the time goes in v2:
time: 125 us
  Pallas kernels  116 us (93%)
  local copies, waits for them, and re-layouts  5.26 us (4%)
  between operations  2.59 us (2%)
  other arithmetic  1.48 us (1%)
    pallas_call x1, Pallas kernels, call_down(): pl.pallas_call(down_kernel, out_shape=jax.ShapeDtypeStruct((64, 128), F32...  36 us
    pallas_call x1, Pallas kernels, call_cross(): pl.pallas_call(functools.partial(cross_kernel, devices), out_shape=(jax.S...  29.8 us
    pallas_call x1, Pallas kernels, call_step(): pl.pallas_call(functools.partial(step_kernel, devices), out_shape=(flat,...  25.6 us
    pallas_call x1, Pallas kernels, call_up(): pl.pallas_call(up_kernel, out_shape=(jax.ShapeDtypeStruct((40, count), F3...  24.6 us
    unnamed x4, local copies, waits for them, and re-layouts  4.64 us

profile of v2, /device:TPU:0, one launch (start us, length us, event | category | flops | bytes accessed | tf_op | source)
XLA Modules:
  0.0 125.3 jit_solution(10864561331618858308)
XLA Ops:
  2.6 0.5 broadcast.3
  3.1 1.5 %reduce.3 = s32[8192]{0:T(1024)S(1)} reduce(s32[1,8192]{1,0:T(1,128)} %param.20, s32[]{:T(128)} %broadcast.3), dimensions={0}, to_apply=%param.20.reduce_sub_computation.3 | reduce | bytes 65540 | tf_op args[6]
  4.6 0.6 reshape.31.perm
  5.2 24.6 %up_tree.1 = (f32[40,8192]{1,0:T(8,128)}, bf16[32,256,128]{2,1,0:T(8,128)(2,1)}, f32[64,256]{1,0:T(8,128)}) custom-call(s32[8192]{0:T(1024)} %bitcast.8, f32[1]{0:T(128)S(6)} %copy.21.rate_ref, f32[32,8192]{1,0:T(8,128)} %pts.1, f32[64,128]{1,0:T(8,128)} %bitcast.9, f32[62,32,256]{2,1,0:T(8,128)} %skel.5, bf16[62,256,256]{2,1,0:T(8,128)(2,1)} %trans.5), custom_call_target="tpu_custom_call" | custom-call | tf_op jit(solution)/shard_map/up_tree/pallas_call | solution.py:242
  29.7 29.8 %cross_levels.1 = (f32[1,256]{1,0:T(1,128)}, f32[40,4096]{1,0:T(8,128)}, f32[40,4096]{1,0:T(8,128)}) custom-call(f32[1]{0:T(128)S(6)} %copy.21.rate_ref, f32[64,256]{1,0:T(8,128)} %get-tuple-element.13.ups, f32[4,2,32,256]{3,2,1,0:T(8,128)} %skel.4, bf16[3,2,256,256]{3,2,1,0:T(8,128)(2,1)} %trans.4, f32[40,8192]{1,0:T(8,128)} %get-tuple-element.12.gt), custom_call_target="tpu_custom_call" | custom-call | tf_op jit(solution)/shard_map/cross_levels/pallas_call | solution.py:392
  59.6 36.0 %down_near.1.image = f32[64,128]{1,0:T(8,128)} custom-call(s32[256]{0:T(256)} %tgt.1, s32[256]{0:T(256)} %src.1, s32[1]{0:T(128)S(6)} %copy.22.cnt, s32[1]{0:T(128)} %bitcast.first_ref, f32[1]{0:T(128)S(6)} %copy.21.rate_ref, f32[1]{0:T(128)S(6)} %copy.20.ridge_ref, s32[32,256]{1,0:T(8,128)} %reshape.31.perm, f32[40,8192]{1,0:T(8,128)} %get-tuple-element.12.gt, ...), custom_call_target="tpu_custom_call" | custom-call | tf_op jit(solution)/shard_map/down_near/pallas_call | solution.py:258
  95.6 25.6 %step.1 = (f32[64,128]{1,0:T(8,128)}, f32[64,128]{1,0:T(8,128)}, f32[64,128]{1,0:T(8,128)}) custom-call(f32[64,128]{1,0:T(8,128)} %down_near.1.image, f32[64,128]{1,0:T(8,128)} %bitcast.14, f32[64,128]{1,0:T(8,128)} %bitcast.15, f32[64,128]{1,0:T(8,128)} %bitcast.10), custom_call_target="tpu_custom_call" | custom-call | tf_op jit(solution)/shard_map/step/pallas_call | solution.py:478
  121.2 1.4 %copy.23 = f32[8192]{0:T(1024)} copy(f32[8192]{0:T(1024)} %bitcast.13) | data formatting | bytes 65536
  122.6 1.4 %copy.24 = f32[8192]{0:T(1024)} copy(f32[8192]{0:T(1024)} %bitcast.12) | data formatting | bytes 65536
  123.9 1.4 %copy.25 = f32[8192]{0:T(1024)} copy(f32[8192]{0:T(1024)} %bitcast.11) | data formatting | bytes 65536

commit v3 on v2

--- a/solution.py
+++ b/solution.py
@@ -37,12 +37,25 @@
     return jnp.sum(pts * pts, axis=0, keepdims=True) * (-rate * LOG2E)
 
 
-def row_stack(pts, norm):
+def row_stack(pts, norm, value):
     high, low = split(pts, 2)
     one = jnp.ones_like(norm)
     width = pts.shape[1]
-    tail = jnp.concatenate(split(norm, 3) + [one] * 3 + [jnp.zeros((26, width), F32)], axis=0)
+    tail = jnp.concatenate(
+        split(norm, 3)
+        + [one] * 3
+        + [jnp.zeros((10, width), F32)]
+        + split(value, 3)
+        + [jnp.zeros((13, width), F32)],
+        axis=0,
+    )
     return jnp.concatenate([high, high, low, tail], axis=0)
+
+
+def value_column(rows):
+    at = lax.broadcasted_iota(jnp.int32, (128, 128), 0)
+    chosen = jnp.where((at >= 112) & (at < 115), 1.0, 0.0).astype(BF16)
+    return jnp.dot(rows, chosen, preferred_element_type=F32)
 
 
 def col_stack(pts, norm, rate):
@@ -70,21 +83,19 @@
     _first, _width = _first + _width, _width // 2
 
 
-def up_kernel(perm, rate_ref, pts, dirs, skel, trans, gt, rows_out, ups, raw, held):
+def order_kernel(perm, rate_ref, pts, dirs, gt, rows_out, raw, held):
     rate = rate_ref[0]
     blocks = pts.shape[1] // 128
 
     def place(block, _):
         at = pl.multiple_of(block * 128, 128)
         part = pts[:, pl.ds(at, 128)]
-        stacked = jnp.concatenate(
-            [part, dirs[pl.ds(block, 1), :], norm_row(part, rate), jnp.zeros((94, 128), F32)],
-            axis=0,
-        )
-        raw[pl.ds(at, 128), :] = stacked.T
-        return 0
-
-    lax.fori_loop(0, blocks, place, 0, unroll=2)
+        raw[pl.ds(at, 128), :] = row_stack(
+            part, norm_row(part, rate), dirs[pl.ds(block, 1), :]
+        ).T
+        return 0
+
+    lax.fori_loop(0, blocks, place, 0, unroll=4)
 
     def gather(group, _):
         base = pl.multiple_of(group * 32, 32)
@@ -97,36 +108,30 @@
     def leaf(j, _):
         at = pl.multiple_of(j * LEAF, LEAF)
         mine = held[pl.ds(at, LEAF), :]
+        rows_out[j] = mine.astype(BF16)
         turned = mine.T
-        gt[:, pl.ds(at, LEAF)] = turned[:40]
-        rows = row_stack(turned[:32], turned[33:34]).T.astype(BF16)
-        rows_out[j] = rows
-        node = skel[j]
-        kern = tile(rows, col_stack(node, norm_row(node, rate), rate))
-        ups[pl.ds(j, 1), :] = jnp.sum(kern * mine[:, 32:33], axis=0, keepdims=True)
-        return 0
-
-    lax.fori_loop(0, LEAVES_DEV, leaf, 0, unroll=2)
-
-    for first, width in LEVELS:
-        for i in range(width // 2):
-            total = jnp.zeros((16, LEAF), F32)
-            for node in (first + 2 * i, first + 2 * i + 1):
-                total = total + jnp.dot(
-                    split_rows(ups[node : node + 1, :]), trans[node], preferred_element_type=F32
-                )
-            ups[first + width + i : first + width + i + 1, :] = (
-                jnp.sum(total, axis=0, keepdims=True) * half_root
-            )
-    ups[63:64, :] = jnp.zeros((1, LEAF), F32)
+        gt[0:32, pl.ds(at, LEAF)] = turned[0:32] + turned[64:96]
+        gt[32:40, pl.ds(at, LEAF)] = jnp.concatenate(
+            [
+                turned[112:113] + turned[113:114] + turned[114:115],
+                turned[96:97] + turned[97:98] + turned[98:99],
+                jnp.zeros((6, LEAF), F32),
+            ],
+            axis=0,
+        )
+        return 0
+
+    lax.fori_loop(0, LEAVES_DEV, leaf, 0, unroll=4)
 
 
 def down_kernel(
-    tgt, src, cnt, first_ref, rate_ref, ridge_ref, perm, gt, left, right, rows, ups, root,
-    skel, trans, image, cols, dirs, acc, couple, turned_img,
+    tgt, src, cnt, first_ref, rate_ref, ridge_ref, perm, gt, left, right, rows, down,
+    skel_hbm, image, cols, dirs, acc, turned_img, skel, skel_sem,
 ):
     rate = rate_ref[0]
     first = first_ref[0]
+    fetch = pltpu.make_async_copy(skel_hbm.at[pl.ds(0, LEAVES_DEV)], skel, skel_sem)
+    fetch.start()
 
     def load_cols(ref, base):
         def body(i, _):
@@ -142,50 +147,16 @@
     load_cols(right, REACH + LEAVES_DEV)
 
     lane = lax.broadcasted_iota(jnp.int32, (LEAF, 128), 1)
-    couple[...] = jnp.zeros_like(couple)
-
-    def pair(i, _):
-        for a, b in ((2 * i, 2 * i + 1), (2 * i + 1, 2 * i)):
-            mine, other = skel[a], skel[b]
-            kern = tile(
-                row_stack(mine, norm_row(mine, rate)).T.astype(BF16),
-                col_stack(other, norm_row(other, rate), rate),
-            )
-            value = jnp.sum(kern * ups[pl.ds(b, 1), :], axis=1, keepdims=True)
-            couple[...] = jnp.where(lane == a, value, couple[...])
-        return 0
-
-    lax.fori_loop(0, NODES // 2, pair, 0)
-    coupled = couple[...].T
-
-    down = {NODES: root[...]}
-    for level in range(len(LEVELS) - 1, -1, -1):
-        start, width = LEVELS[level]
-        for i in range(width // 2):
-            parts = split_rows(down[start + width + i])
-            for node in (start + 2 * i, start + 2 * i + 1):
-                moved = lax.dot_general(
-                    parts, trans[node], (((1,), (1,)), ((), ())), preferred_element_type=F32
-                )
-                down[node] = coupled[node : node + 1] + jnp.sum(moved, axis=0, keepdims=True)
-    couple[0:LEAVES_DEV, :] = jnp.concatenate(
-        [down[j][:, 0:128] for j in range(LEAVES_DEV)], axis=0
-    )
-    couple[LEAVES_DEV : 2 * LEAVES_DEV, :] = jnp.concatenate(
-        [down[j][:, 128:256] for j in range(LEAVES_DEV)], axis=0
-    )
-
     def far(j, _):
         node = skel[j]
         kern = tile(rows[j], col_stack(node, norm_row(node, rate), rate))
-        acc[0, j] = (
-            kern[:, 0:128] * couple[pl.ds(j, 1), :]
-            + kern[:, 128:256] * couple[pl.ds(j + LEAVES_DEV, 1), :]
-        )
+        kern = kern * down[pl.ds(j, 1), :]
+        acc[0, j] = kern[:, 0:128] + kern[:, 128:256]
         for way in range(1, WAYS):
             acc[way, j] = jnp.zeros((LEAF, 128), F32)
         return 0
 
+    fetch.wait()
     lax.fori_loop(0, LEAVES_DEV, far, 0, unroll=2)
 
     total = cnt[0]
@@ -237,39 +208,39 @@
 PARAMS = pltpu.CompilerParams(vmem_limit_bytes=60 * 1024 * 1024)
 
 
-def call_up(perm, rate, points, direction, skeleton, transfer):
+def call_order(perm, rate, points, direction):
     count = points.shape[1]
     return pl.pallas_call(
-        up_kernel,
+        order_kernel,
         out_shape=(
             jax.ShapeDtypeStruct((40, count), F32),
             jax.ShapeDtypeStruct((LEAVES_DEV, LEAF, 128), BF16),
-            jax.ShapeDtypeStruct((64, LEAF), F32),
         ),
-        in_specs=[SMEM, SMEM, VMEM, VMEM, VMEM, VMEM],
-        out_specs=(VMEM, VMEM, VMEM),
+        in_specs=[SMEM, SMEM, VMEM, VMEM],
+        out_specs=(VMEM, VMEM),
         scratch_shapes=[pltpu.VMEM((count, 128), F32), pltpu.VMEM((count, 128), F32)],
         compiler_params=PARAMS,
-        name="up_tree",
-    )(perm, rate, points, direction, skeleton, transfer)
-
-
-def call_down(tgt, src, cnt, first, rate, ridge, perm, gt, left, right, rows, ups, root, skel, trans):
+        name="tree_order",
+    )(perm, rate, points, direction)
+
+
+def call_down(tgt, src, cnt, first, rate, ridge, perm, gt, left, right, rows, down, skel):
     return pl.pallas_call(
         down_kernel,
         out_shape=jax.ShapeDtypeStruct((64, 128), F32),
-        in_specs=[SMEM] * 6 + [VMEM] * 9,
+        in_specs=[SMEM] * 6 + [VMEM] * 6 + [pl.BlockSpec(memory_space=pl.ANY)],
         out_specs=VMEM,
         scratch_shapes=[
             pltpu.VMEM((LEAVES_DEV + 2 * REACH, 128, LEAF), BF16),
             pltpu.VMEM((LEAVES_DEV + 2 * REACH, 8, LEAF), F32),
             pltpu.VMEM((WAYS, LEAVES_DEV, LEAF, 128), F32),
             pltpu.VMEM((LEAF, 128), F32),
-            pltpu.VMEM((LEAF, 128), F32),
+            pltpu.VMEM((LEAVES_DEV, DIM, LEAF), F32),
+            pltpu.SemaphoreType.DMA,
         ],
         compiler_params=PARAMS,
-        name="down_near",
-    )(tgt, src, cnt, first, rate, ridge, perm, gt, left, right, rows, ups, root, skel, trans)
+        name="near_far",
+    )(tgt, src, cnt, first, rate, ridge, perm, gt, left, right, rows, down, skel)
 
 
 def remote_params(collective_id):
@@ -296,8 +267,9 @@
 
 
 def cross_kernel(
-    devices, rate_ref, ups, skel, trans, gt, down, left, right,
-    sent, slots, kerns, couple, halo_send, halo_recv, hop_send, hop_recv,
+    devices, rate_ref, rows, local_skel, skel, trans, local_hbm, gt, down_out, left, right,
+    ups, coupled, local, columns, sent, slots, kerns, couple,
+    halo_send, halo_recv, hop_send, hop_recv, local_sem,
 ):
     rate = rate_ref[0]
     me = lax.axis_index("leaf")
@@ -309,6 +281,8 @@
         peers.append(me + mask * (1 - 2 * ((me // mask) % 2)))
     has_left, has_right = me > 0, me < devices - 1
 
+    fetch = pltpu.make_async_copy(local_hbm, local, local_sem)
+    fetch.start()
     barrier = pltpu.get_barrier_semaphore()
     for peer in peers:
         signal(barrier, peer)
@@ -334,22 +308,79 @@
         gt.at[:, pl.ds(gt.shape[1] - edge, edge)], left, halo_send.at[1], halo_recv.at[1], me + 1
     )
 
+    pl.when(has_left)(to_left.start)
+    pl.when(has_right)(to_right.start)
+
+    def leaf(j, _):
+        node = local_skel[j]
+        mine = rows[j]
+        kern = tile(mine, col_stack(node, norm_row(node, rate), rate))
+        value = value_column(mine)
+        ups[pl.ds(j, 1), :] = jnp.concatenate(
+            [
+                jnp.sum(kern[:, 0:128] * value, axis=0, keepdims=True),
+                jnp.sum(kern[:, 128:256] * value, axis=0, keepdims=True),
+            ],
+            axis=1,
+        )
+        return 0
+
+    lax.fori_loop(0, LEAVES_DEV, leaf, 0, unroll=4)
+    fetch.wait()
+    for first, width in LEVELS:
+        for i in range(width // 2):
+            total = jnp.zeros((16, LEAF), F32)
+            for node in (first + 2 * i, first + 2 * i + 1):
+                total = total + jnp.dot(
+                    split_rows(ups[node : node + 1, :]), local[node], preferred_element_type=F32
+                )
+            ups[first + width + i : first + width + i + 1, :] = (
+                jnp.sum(total, axis=0, keepdims=True) * half_root
+            )
+
     current = ups[NODES : NODES + 1, :]
     sent[0] = jnp.broadcast_to(current, (8, LEAF))
     hop(0).start()
-    pl.when(has_left)(to_left.start)
-    pl.when(has_right)(to_right.start)
+
+    lane = lax.broadcasted_iota(jnp.int32, (LEAF, 128), 1)
+    columns[...] = jnp.zeros_like(columns)
+
+    def pair(i, _):
+        a, b = 2 * i, 2 * i + 1
+        mine, other = local_skel[a], local_skel[b]
+        up_a, up_b = ups[pl.ds(a, 1), :], ups[pl.ds(b, 1), :]
+        mine_rows = row_stack(mine, norm_row(mine, rate), up_a).T.astype(BF16)
+        kern = tile(mine_rows, col_stack(other, norm_row(other, rate), rate))
+        value = value_column(mine_rows)
+        coupled[pl.ds(b, 1), :] = jnp.concatenate(
+            [
+                jnp.sum(kern[:, 0:128] * value, axis=0, keepdims=True),
+                jnp.sum(kern[:, 128:256] * value, axis=0, keepdims=True),
+            ],
+            axis=1,
+        )
+        columns[...] = jnp.where(
+            lane == a, jnp.sum(kern * up_b, axis=1, keepdims=True), columns[...]
+        )
+        return 0
 
     def couplings(level, _):
         mine, other = skel[level, 0], skel[level, 1]
+        norm = norm_row(mine, rate)
         kerns[level] = tile(
-            row_stack(mine, norm_row(mine, rate)).T.astype(BF16),
+            row_stack(mine, norm, norm).T.astype(BF16),
             col_stack(other, norm_row(other, rate), rate),
         )
         return 0
 
-    lax.fori_loop(0, levels, couplings, 0)
+    pairs = NODES // 2
+    share = (pairs + levels - 1) // levels
     for level in range(levels):
+        lax.fori_loop(
+            min(share * level, pairs), min(share * (level + 1), pairs), pair, 0, unroll=2
+        )
+        if level == levels - 2:
+            lax.fori_loop(0, levels, couplings, 0, unroll=2)
         hop(level).wait()
         if level < levels - 1:
             total = jnp.dot(
@@ -360,7 +391,6 @@
             current = jnp.sum(total, axis=0, keepdims=True) * half_root
             sent[level + 1] = jnp.broadcast_to(current, (8, LEAF))
             hop(level + 1).start()
-    lane = lax.broadcasted_iota(jnp.int32, (LEAF, 128), 1)
     picked = jnp.zeros((LEAF, 128), F32)
     for level in range(levels):
         value = jnp.sum(kerns[level] * slots[level][0:1], axis=1, keepdims=True)
@@ -373,7 +403,20 @@
             preferred_element_type=F32,
         )
         current = couple[level : level + 1, :] + jnp.sum(moved, axis=0, keepdims=True)
-    down[...] = current
+    turned = columns[...].T
+    down = {NODES: current}
+    for level in range(len(LEVELS) - 1, -1, -1):
+        start, width = LEVELS[level]
+        for i in range(width // 2):
+            parts = split_rows(down[start + width + i])
+            for node in (start + 2 * i, start + 2 * i + 1):
+                moved = lax.dot_general(
+                    parts, local[node], (((1,), (1,)), ((), ())), preferred_element_type=F32
+                )
+                own = coupled[node : node + 1, :] if node % 2 else turned[node : node + 1]
+                down[node] = own + jnp.sum(moved, axis=0, keepdims=True)
+    for node in range(LEAVES_DEV):
+        down_out[node : node + 1, :] = down[node]
 
     @pl.when(has_left)
     def _():
@@ -386,21 +429,24 @@
         to_left.wait_recv()
 
 
-def call_cross(devices, rate, ups, skel, trans, gt):
+def call_cross(devices, rate, rows, local_skel, skel, trans, local_trans, gt):
     levels = skel.shape[0]
     edge = REACH * LEAF
+    far = pl.BlockSpec(memory_space=pl.ANY)
     return pl.pallas_call(
         functools.partial(cross_kernel, devices),
         out_shape=(
-            jax.ShapeDtypeStruct((1, LEAF), F32),
+            jax.ShapeDtypeStruct((LEAVES_DEV, LEAF), F32),
             jax.ShapeDtypeStruct((40, edge), F32),
             jax.ShapeDtypeStruct((40, edge), F32),
         ),
-        in_specs=[SMEM, VMEM, VMEM, VMEM, pl.BlockSpec(memory_space=pl.ANY)],
-        out_specs=(
-            VMEM, pl.BlockSpec(memory_space=pl.ANY), pl.BlockSpec(memory_space=pl.ANY),
-        ),
+        in_specs=[SMEM, VMEM, VMEM, VMEM, VMEM, far, far],
+        out_specs=(VMEM, far, far),
         scratch_shapes=[
+            pltpu.VMEM((64, LEAF), F32),
+            pltpu.VMEM((64, LEAF), F32),
+            pltpu.VMEM(local_trans.shape, BF16),
+            pltpu.VMEM((LEAF, 128), F32),
             pltpu.VMEM((levels, 8, LEAF), F32),
             pltpu.VMEM((levels, 8, LEAF), F32),
             pltpu.VMEM((levels, LEAF, LEAF), F32),
@@ -409,15 +455,15 @@
             pltpu.SemaphoreType.DMA((2,)),
             pltpu.SemaphoreType.DMA((levels,)),
             pltpu.SemaphoreType.DMA((levels,)),
+            pltpu.SemaphoreType.DMA,
         ],
         compiler_params=remote_params(0),
-        name="cross_levels",
-    )(rate, ups, skel, trans, gt)
+        name="tree",
+    )(rate, rows, local_skel, skel, trans, local_trans, gt)
 
 
 def step_kernel(
-    devices, image, solution, residual, direction, new_solution, new_residual, new_direction,
-    sent, slots, send_sem, recv_sem,
+    devices, image, residual, direction, factors, sent, slots, send_sem, recv_sem,
 ):
     me = lax.axis_index("leaf")
     barrier = pltpu.get_barrier_semaphore()
@@ -464,22 +510,37 @@
     norm_old = sums[0:1]
     step_size = norm_old / sums[1:2]
     new_res = res - step_size * img
-    new_residual[...] = new_res
     sent[1] = jnp.concatenate(
         [jnp.sum(new_res * new_res, axis=0, keepdims=True), jnp.zeros((7, 128), F32)], axis=0
     )
     norm_new = total(1)[0:1]
+    factors[...] = jnp.concatenate(
+        [
+            jnp.broadcast_to(step_size, (8, 128)),
+            jnp.broadcast_to(norm_new / (norm_old + epsilon), (8, 128)),
+        ],
+        axis=0,
+    )
+
+
+def update_kernel(
+    factors, image, solution, residual, direction, new_solution, new_residual, new_direction
+):
+    step_size, turn = factors[0:1, :], factors[8:9, :]
+    dire = direction[...]
+    new_res = residual[...] - step_size * image[...]
+    new_residual[...] = new_res
     new_solution[...] = solution[...] + step_size * dire
-    new_direction[...] = new_res + norm_new / (norm_old + epsilon) * dire
+    new_direction[...] = new_res + turn * dire
 
 
 def call_step(devices, image, solution, residual, direction):
     flat = jax.ShapeDtypeStruct((64, 128), F32)
-    return pl.pallas_call(
+    factors = pl.pallas_call(
         functools.partial(step_kernel, devices),
-        out_shape=(flat, flat, flat),
-        in_specs=[VMEM] * 4,
-        out_specs=(VMEM,) * 3,
+        out_shape=jax.ShapeDtypeStruct((16, 128), F32),
+        in_specs=[VMEM] * 3,
+        out_specs=VMEM,
         scratch_shapes=[
             pltpu.VMEM((2, 8, 128), F32),
             pltpu.VMEM((2, devices, 8, 128), F32),
@@ -488,7 +549,14 @@
         ],
         compiler_params=remote_params(1),
         name="step",
-    )(image, solution, residual, direction)
+    )(image, residual, direction)
+    return pl.pallas_call(
+        update_kernel,
+        out_shape=(flat, flat, flat),
+        in_specs=[VMEM] * 5,
+        out_specs=(VMEM,) * 3,
+        name="update",
+    )(factors, image, solution, residual, direction)
 
 
 def shards(
@@ -509,17 +577,15 @@
 ):
     devices = lax.axis_size("leaf")
     folded = tuple(array.reshape(64, 128) for array in (solution, residual, direction))
-    gt, rows, ups = call_up(
-        tree_perm[0], kernel_rate, points, folded[2], local_skeleton, local_transfer
-    )
-    root, left, right = call_cross(
-        devices, kernel_rate, ups, cross_skeleton, cross_transfer, gt
+    gt, rows = call_order(tree_perm[0], kernel_rate, points, folded[2])
+    down, left, right = call_cross(
+        devices, kernel_rate, rows, local_skeleton, cross_skeleton, cross_transfer,
+        local_transfer, gt,
     )
     own_first = (lax.axis_index("leaf") * LEAVES_DEV).astype(jnp.int32).reshape(1)
     image = call_down(
         near_target, near_source, tile_count, own_first, kernel_rate, ridge_weight,
-        tree_perm.reshape(LEAVES_DEV, LEAF), gt, left, right, rows, ups, root,
-        local_skeleton, local_transfer,
+        tree_perm.reshape(LEAVES_DEV, LEAF), gt, left, right, rows, down, local_skeleton,
     )
     return tuple(array.reshape(-1) for array in call_step(devices, image, *folded))
 

time: 125 us -> 99.7 us (0.80)
  Pallas kernels: 116 us -> 94 us
  local copies, waits for them, and re-layouts: 5.26 us -> 1.14 us
    pallas_call x1, Pallas kernels: 36 us -> 19.4 us  [call_down(): pl.pallas_call(down_kernel, out_shape=jax.ShapeDtypeStruct((64, 128), F32...]
    pallas_call x2 -> x3, Pallas kernels: 50.1 us -> 41.3 us  [the longest x1 25.9 us: call_step(): pl.pallas_call(functools.partial(step_kernel, devices), out_shape=jax.Sha...]
    unnamed x4 -> x1, local copies, waits for them, and re-layouts: 4.64 us -> 0.51 us
    pallas_call x1, Pallas kernels: 29.8 us -> 33.3 us  [call_cross(): pl.pallas_call(functools.partial(cross_kernel, devices), out_shape=(jax.S...]
where the time goes in v3:
time: 99.7 us; the launch traced here: 99.2 us
  Pallas kernels  94 us (94%)
  between operations  2.6 us (3%)
  other arithmetic  1.48 us (1%)
  local copies, waits for them, and re-layouts  1.14 us (1%)
    pallas_call x1, Pallas kernels, call_cross(): pl.pallas_call(functools.partial(cross_kernel, devices), out_shape=(jax.S...  33.3 us
    pallas_call x1, Pallas kernels, call_step(): pl.pallas_call(functools.partial(step_kernel, devices), out_shape=jax.Sha...  25.9 us
    pallas_call x1, Pallas kernels, call_down(): pl.pallas_call(down_kernel, out_shape=jax.ShapeDtypeStruct((64, 128), F32...  19.4 us
    pallas_call x1, Pallas kernels, call_order(): pl.pallas_call(order_kernel, out_shape=(jax.ShapeDtypeStruct((40, count),...  13.9 us

profile of v3, /device:TPU:0, one launch (start us, length us, event | category | flops | bytes accessed | tf_op | source)
XLA Modules:
  0.0 99.2 jit_solution(8683568100442986659)
XLA Ops:
  2.6 0.5 broadcast.3
  3.1 1.5 %reduce.3 = s32[8192]{0:T(1024)S(1)} reduce(s32[1,8192]{1,0:T(1,128)} %param.20, s32[]{:T(128)} %broadcast.3), dimensions={0}, to_apply=%param.20.reduce_sub_computation.3 | reduce | bytes 65540 | tf_op args[6]
  4.6 0.6 reshape.31.perm
  5.2 13.9 %tree_order.1 = (f32[40,8192]{1,0:T(8,128)}, bf16[32,256,128]{2,1,0:T(8,128)(2,1)}) custom-call(s32[8192]{0:T(1024)} %bitcast.11, f32[1]{0:T(128)S(6)} %copy.18.rate_ref, f32[32,8192]{1,0:T(8,128)} %pts.1, f32[64,128]{1,0:T(8,128)} %bitcast.8), custom_call_target="tpu_custom_call" | custom-call | tf_op jit(solution)/shard_map/tree_order/pallas_call | solution.py:213
  19.1 33.3 %tree.1 = (f32[32,256]{1,0:T(8,128)}, f32[40,4096]{1,0:T(8,128)}, f32[40,4096]{1,0:T(8,128)}) custom-call(f32[1]{0:T(128)S(6)} %copy.18.rate_ref, bf16[32,256,128]{2,1,0:T(8,128)(2,1)} %get-tuple-element.12.rows, f32[62,32,256]{2,1,0:T(8,128)} %skel_hbm.1, f32[4,2,32,256]{3,2,1,0:T(8,128)} %skel.1, bf16[3,2,256,256]{3,2,1,0:T(8,128)(2,1)} %trans.1, ...), custom_call_target="tpu_custom_call" | custom-call | tf_op jit(solution)/shard_map/tree/pallas_call | solution.py:436
  52.4 19.4 %near_far.1.image = f32[64,128]{1,0:T(8,128)} custom-call(s32[256]{0:T(256)} %tgt.1, s32[256]{0:T(256)} %src.1, s32[1]{0:T(128)S(6)} %copy.19.cnt, s32[1]{0:T(128)} %bitcast.first_ref, f32[1]{0:T(128)S(6)} %copy.18.rate_ref, f32[1]{0:T(128)S(6)} %copy.17.ridge_ref, s32[32,256]{1,0:T(8,128)} %reshape.31.perm, f32[40,8192]{1,0:T(8,128)} %get-tuple-element.11.gt, ...), custom_call_target="tpu_custom_call" | custom-call | tf_op jit(solution)/shard_map/near_far/pallas_call | solution.py:228
  71.9 25.9 %step.1.factors = f32[16,128]{1,0:T(8,128)} custom-call(f32[64,128]{1,0:T(8,128)} %near_far.1.image, f32[64,128]{1,0:T(8,128)} %bitcast.12, f32[64,128]{1,0:T(8,128)} %bitcast.9), custom_call_target="tpu_custom_call" | custom-call | tf_op jit(solution)/shard_map/step/pallas_call | solution.py:539
  97.8 1.5 %update.1 = (f32[64,128]{1,0:T(8,128)}, f32[64,128]{1,0:T(8,128)}, f32[64,128]{1,0:T(8,128)}) custom-call(f32[16,128]{1,0:T(8,128)} %step.1.factors, f32[64,128]{1,0:T(8,128)} %near_far.1.image, f32[64,128]{1,0:T(8,128)} %bitcast.14, f32[64,128]{1,0:T(8,128)} %bitcast.13, f32[64,128]{1,0:T(8,128)} %bitcast.10), custom_call_target="tpu_custom_call" | custom-call | tf_op jit(solution)/shard_map/update/pallas_call | solution.py:553

commit v4 on v3

--- a/solution.py
+++ b/solution.py
@@ -13,7 +13,8 @@
 REACH = 16
 DIM = 32
 NODES = 62
-WAYS = 4
+WAYS = 8
+SUMS = 2
 
 epsilon = 1e-06
 half_root = 0.5**0.5
@@ -83,7 +84,7 @@
     _first, _width = _first + _width, _width // 2
 
 
-def order_kernel(perm, rate_ref, pts, dirs, gt, rows_out, raw, held):
+def order_kernel(perm, rate_ref, pts, dirs, gt, dir_out, rows_out, raw, held):
     rate = rate_ref[0]
     blocks = pts.shape[1] // 128
 
@@ -100,51 +101,52 @@
     def gather(group, _):
         base = pl.multiple_of(group * 32, 32)
         for i in range(32):
-            held[pl.ds(base + i, 1), :] = raw[pl.ds(perm[base + i], 1), :]
+            held[pl.ds(base + i, 1), :] = raw[pl.ds(perm[0, base + i], 1), :]
         return 0
 
     lax.fori_loop(0, pts.shape[1] // 32, gather, 0)
+
+    to = lax.broadcasted_iota(jnp.int32, (48, 128), 0)
+    of = lax.broadcasted_iota(jnp.int32, (48, 128), 1)
+    point = (to < DIM) & ((of == to) | (of == to + 64))
+    value = (to == DIM) & (of >= 112) & (of < 115)
+    chosen = jnp.where(point | value, 1.0, 0.0).astype(BF16)
 
     def leaf(j, _):
         at = pl.multiple_of(j * LEAF, LEAF)
-        mine = held[pl.ds(at, LEAF), :]
-        rows_out[j] = mine.astype(BF16)
-        turned = mine.T
-        gt[0:32, pl.ds(at, LEAF)] = turned[0:32] + turned[64:96]
-        gt[32:40, pl.ds(at, LEAF)] = jnp.concatenate(
-            [
-                turned[112:113] + turned[113:114] + turned[114:115],
-                turned[96:97] + turned[97:98] + turned[98:99],
-                jnp.zeros((6, LEAF), F32),
-            ],
-            axis=0,
-        )
+        mine = held[pl.ds(at, LEAF), :].astype(BF16)
+        rows_out[j] = mine
+        turned = lax.dot_general(
+            chosen, mine, (((1,), (1,)), ((), ())), preferred_element_type=F32
+        )
+        gt[:, pl.ds(at, LEAF)] = turned[0:DIM]
+        dir_out[pl.ds(j, 1), :] = turned[DIM : DIM + 1]
         return 0
 
     lax.fori_loop(0, LEAVES_DEV, leaf, 0, unroll=4)
 
 
 def down_kernel(
-    tgt, src, cnt, first_ref, rate_ref, ridge_ref, perm, gt, left, right, rows, down,
-    skel_hbm, image, cols, dirs, acc, turned_img, skel, skel_sem,
+    tgt, src, cnt, first_ref, rate_ref, ridge_ref, perm, gt, own_dir, left, left_dir,
+    right, right_dir, rows, down, skel_hbm, image, cols, dirs, acc, turned_img, skel, skel_sem,
 ):
     rate = rate_ref[0]
     first = first_ref[0]
     fetch = pltpu.make_async_copy(skel_hbm.at[pl.ds(0, LEAVES_DEV)], skel, skel_sem)
     fetch.start()
 
-    def load_cols(ref, base):
+    def load_cols(ref, dir_ref, base):
         def body(i, _):
-            at = pl.multiple_of(i * LEAF, LEAF)
-            cols[base + i] = col_stack(ref[0:32, pl.ds(at, LEAF)], ref[33:34, pl.ds(at, LEAF)], rate)
-            dirs[base + i] = jnp.broadcast_to(ref[32:33, pl.ds(at, LEAF)], (8, LEAF))
+            part = ref[:, pl.ds(pl.multiple_of(i * LEAF, LEAF), LEAF)]
+            cols[base + i] = col_stack(part, norm_row(part, rate), rate)
+            dirs[base + i] = jnp.broadcast_to(dir_ref[pl.ds(i, 1), :], (8, LEAF))
             return 0
 
-        lax.fori_loop(0, ref.shape[1] // LEAF, body, 0, unroll=2)
-
-    load_cols(left, 0)
-    load_cols(gt, REACH)
-    load_cols(right, REACH + LEAVES_DEV)
+        lax.fori_loop(0, ref.shape[1] // LEAF, body, 0, unroll=4)
+
+    load_cols(left, left_dir, 0)
+    load_cols(gt, own_dir, REACH)
+    load_cols(right, right_dir, REACH + LEAVES_DEV)
 
     lane = lax.broadcasted_iota(jnp.int32, (LEAF, 128), 1)
     def far(j, _):
@@ -152,7 +154,7 @@
         kern = tile(rows[j], col_stack(node, norm_row(node, rate), rate))
         kern = kern * down[pl.ds(j, 1), :]
         acc[0, j] = kern[:, 0:128] + kern[:, 128:256]
-        for way in range(1, WAYS):
+        for way in range(1, SUMS):
             acc[way, j] = jnp.zeros((LEAF, 128), F32)
         return 0
 
@@ -169,7 +171,7 @@
             source = jnp.where(slot < total, source, target + REACH)
             weight = jnp.where(slot < total, dirs[source][0:1, :], 0.0)
             kern = tile(rows[target], cols[source]) * weight
-            acc[way, target] += kern[:, 0:128] + kern[:, 128:256]
+            acc[way % SUMS, target] += kern[:, 0:128] + kern[:, 128:256]
         return 0
 
     lax.fori_loop(0, (total + WAYS - 1) // WAYS, near, 0)
@@ -178,7 +180,7 @@
 
     def gather_image(j, _):
         value = acc[0, j]
-        for way in range(1, WAYS):
+        for way in range(1, SUMS):
             value = value + acc[way, j]
         turned_img[...] = jnp.where(
             lane == j, jnp.sum(value, axis=1, keepdims=True), turned_img[...]
@@ -213,34 +215,35 @@
     return pl.pallas_call(
         order_kernel,
         out_shape=(
-            jax.ShapeDtypeStruct((40, count), F32),
+            jax.ShapeDtypeStruct((DIM, count), F32),
+            jax.ShapeDtypeStruct((LEAVES_DEV, LEAF), F32),
             jax.ShapeDtypeStruct((LEAVES_DEV, LEAF, 128), BF16),
         ),
         in_specs=[SMEM, SMEM, VMEM, VMEM],
-        out_specs=(VMEM, VMEM),
+        out_specs=(VMEM, VMEM, VMEM),
         scratch_shapes=[pltpu.VMEM((count, 128), F32), pltpu.VMEM((count, 128), F32)],
         compiler_params=PARAMS,
         name="tree_order",
     )(perm, rate, points, direction)
 
 
-def call_down(tgt, src, cnt, first, rate, ridge, perm, gt, left, right, rows, down, skel):
+def call_down(tgt, src, cnt, first, rate, ridge, perm, *arrays):
     return pl.pallas_call(
         down_kernel,
         out_shape=jax.ShapeDtypeStruct((64, 128), F32),
-        in_specs=[SMEM] * 6 + [VMEM] * 6 + [pl.BlockSpec(memory_space=pl.ANY)],
+        in_specs=[SMEM] * 6 + [VMEM] * 9 + [pl.BlockSpec(memory_space=pl.ANY)],
         out_specs=VMEM,
         scratch_shapes=[
             pltpu.VMEM((LEAVES_DEV + 2 * REACH, 128, LEAF), BF16),
             pltpu.VMEM((LEAVES_DEV + 2 * REACH, 8, LEAF), F32),
-            pltpu.VMEM((WAYS, LEAVES_DEV, LEAF, 128), F32),
+            pltpu.VMEM((SUMS, LEAVES_DEV, LEAF, 128), F32),
             pltpu.VMEM((LEAF, 128), F32),
             pltpu.VMEM((LEAVES_DEV, DIM, LEAF), F32),
             pltpu.SemaphoreType.DMA,
         ],
         compiler_params=PARAMS,
         name="near_far",
-    )(tgt, src, cnt, first, rate, ridge, perm, gt, left, right, rows, down, skel)
+    )(tgt, src, cnt, first, rate, ridge, perm, *arrays)
 
 
 def remote_params(collective_id):
@@ -267,7 +270,8 @@
 
 
 def cross_kernel(
-    devices, rate_ref, rows, local_skel, skel, trans, local_hbm, gt, down_out, left, right,
+    devices, rate_ref, rows, local_skel, skel, trans, local_hbm, gt, own_dir,
+    down_out, left, left_dir, right, right_dir,
     ups, coupled, local, columns, sent, slots, kerns, couple,
     halo_send, halo_recv, hop_send, hop_recv, local_sem,
 ):
@@ -301,15 +305,30 @@
             sent.at[level], slots.at[level], hop_send.at[level], hop_recv.at[level], peers[level]
         )
 
-    to_left = remote(
-        gt.at[:, pl.ds(0, edge)], right, halo_send.at[0], halo_recv.at[0], me - 1
-    )
-    to_right = remote(
-        gt.at[:, pl.ds(gt.shape[1] - edge, edge)], left, halo_send.at[1], halo_recv.at[1], me + 1
-    )
-
-    pl.when(has_left)(to_left.start)
-    pl.when(has_right)(to_right.start)
+    to_left = (
+        remote(gt.at[:, pl.ds(0, edge)], right, halo_send.at[0], halo_recv.at[0], me - 1),
+        remote(own_dir.at[pl.ds(0, REACH)], right_dir, halo_send.at[1], halo_recv.at[1], me - 1),
+    )
+    to_right = (
+        remote(
+            gt.at[:, pl.ds(gt.shape[1] - edge, edge)], left, halo_send.at[2], halo_recv.at[2],
+            me + 1,
+        ),
+        remote(
+            own_dir.at[pl.ds(LEAVES_DEV - REACH, REACH)], left_dir, halo_send.at[3],
+            halo_recv.at[3], me + 1,
+        ),
+    )
+
+    @pl.when(has_left)
+    def _():
+        for copy in to_left:
+            copy.start()
+
+    @pl.when(has_right)
+    def _():
+        for copy in to_right:
+            copy.start()
 
     def leaf(j, _):
         node = local_skel[j]
@@ -420,16 +439,18 @@
 
     @pl.when(has_left)
     def _():
-        to_left.wait_send()
-        to_right.wait_recv()
+        for out, back in zip(to_left, to_right):
+            out.wait_send()
+            back.wait_recv()
 
     @pl.when(has_right)
     def _():
-        to_right.wait_send()
-        to_left.wait_recv()
-
-
-def call_cross(devices, rate, rows, local_skel, skel, trans, local_trans, gt):
+        for out, back in zip(to_right, to_left):
+            out.wait_send()
+            back.wait_recv()
+
+
+def call_cross(devices, rate, rows, local_skel, skel, trans, local_trans, gt, own_dir):
     levels = skel.shape[0]
     edge = REACH * LEAF
     far = pl.BlockSpec(memory_space=pl.ANY)
@@ -437,11 +458,13 @@
         functools.partial(cross_kernel, devices),
         out_shape=(
             jax.ShapeDtypeStruct((LEAVES_DEV, LEAF), F32),
-            jax.ShapeDtypeStruct((40, edge), F32),
-            jax.ShapeDtypeStruct((40, edge), F32),
+            jax.ShapeDtypeStruct((DIM, edge), F32),
+            jax.ShapeDtypeStruct((REACH, LEAF), F32),
+            jax.ShapeDtypeStruct((DIM, edge), F32),
+            jax.ShapeDtypeStruct((REACH, LEAF), F32),
         ),
-        in_specs=[SMEM, VMEM, VMEM, VMEM, VMEM, far, far],
-        out_specs=(VMEM, far, far),
+        in_specs=[SMEM, VMEM, VMEM, VMEM, VMEM, far, far, far],
+        out_specs=(VMEM, far, far, far, far),
         scratch_shapes=[
             pltpu.VMEM((64, LEAF), F32),
             pltpu.VMEM((64, LEAF), F32),
@@ -451,15 +474,15 @@
             pltpu.VMEM((levels, 8, LEAF), F32),
             pltpu.VMEM((levels, LEAF, LEAF), F32),
             pltpu.VMEM((128, LEAF), F32),
-            pltpu.SemaphoreType.DMA((2,)),
-            pltpu.SemaphoreType.DMA((2,)),
+            pltpu.SemaphoreType.DMA((4,)),
+            pltpu.SemaphoreType.DMA((4,)),
             pltpu.SemaphoreType.DMA((levels,)),
             pltpu.SemaphoreType.DMA((levels,)),
             pltpu.SemaphoreType.DMA,
         ],
         compiler_params=remote_params(0),
         name="tree",
-    )(rate, rows, local_skel, skel, trans, local_trans, gt)
+    )(rate, rows, local_skel, skel, trans, local_trans, gt, own_dir)
 
 
 def step_kernel(
@@ -577,15 +600,16 @@
 ):
     devices = lax.axis_size("leaf")
     folded = tuple(array.reshape(64, 128) for array in (solution, residual, direction))
-    gt, rows = call_order(tree_perm[0], kernel_rate, points, folded[2])
-    down, left, right = call_cross(
+    gt, own_dir, rows = call_order(tree_perm, kernel_rate, points, folded[2])
+    down, left, left_dir, right, right_dir = call_cross(
         devices, kernel_rate, rows, local_skeleton, cross_skeleton, cross_transfer,
-        local_transfer, gt,
+        local_transfer, gt, own_dir,
     )
     own_first = (lax.axis_index("leaf") * LEAVES_DEV).astype(jnp.int32).reshape(1)
     image = call_down(
         near_target, near_source, tile_count, own_first, kernel_rate, ridge_weight,
-        tree_perm.reshape(LEAVES_DEV, LEAF), gt, left, right, rows, down, local_skeleton,
+        tree_perm.reshape(LEAVES_DEV, LEAF), gt, own_dir, left, left_dir,
+        right, right_dir, rows, down, local_skeleton,
     )
     return tuple(array.reshape(-1) for array in call_step(devices, image, *folded))
 

time: 99.7 us -> 90.7 us (0.910)
  Pallas kernels: 94 us -> 85.6 us
    pallas_call x1, Pallas kernels: 25.9 us -> 21.6 us  [call_step(): pl.pallas_call(functools.partial(step_kernel, devices), out_shape=jax.Sha...]
    pallas_call x1, Pallas kernels: 33.3 us -> 30.9 us  [call_cross(): pl.pallas_call(functools.partial(cross_kernel, devices), out_shape=(jax.S...]
    pallas_call x1, Pallas kernels: 19.4 us -> 17.6 us  [call_down(): pl.pallas_call(down_kernel, out_shape=jax.ShapeDtypeStruct((64, 128), F32...]
where the time goes in v4:
time: 90.7 us; the launch traced here: 90.8 us
  Pallas kernels  85.6 us (94%)
  between operations  2.6 us (3%)
  other arithmetic  1.48 us (2%)
  local copies, waits for them, and re-layouts  1.14 us (1%)
    pallas_call x1, Pallas kernels, call_cross(): pl.pallas_call(functools.partial(cross_kernel, devices), out_shape=(jax.S...  30.9 us
    pallas_call x1, Pallas kernels, call_step(): pl.pallas_call(functools.partial(step_kernel, devices), out_shape=jax.Sha...  21.6 us
    pallas_call x1, Pallas kernels, call_down(): pl.pallas_call(down_kernel, out_shape=jax.ShapeDtypeStruct((64, 128), F32...  17.6 us
    pallas_call x1, Pallas kernels, call_order(): pl.pallas_call(order_kernel, out_shape=(jax.ShapeDtypeStruct((DIM, count)...  14 us

profile of v4, /device:TPU:0, one launch (start us, length us, event | category | flops | bytes accessed | tf_op | source)
XLA Modules:
  0.0 90.8 jit_solution(3683264738093611648)
XLA Ops:
  2.6 0.5 broadcast.3
  3.1 1.5 %reduce.3 = s32[8192]{0:T(1024)S(1)} reduce(s32[1,8192]{1,0:T(1,128)} %perm.1, s32[]{:T(128)} %broadcast.3), dimensions={0}, to_apply=%param.20.reduce_sub_computation.3 | reduce | bytes 65540 | tf_op args[6]
  4.6 0.6 reshape.31.perm
  5.2 14.0 %tree_order.1 = (f32[32,8192]{1,0:T(8,128)}, f32[32,256]{1,0:T(8,128)}, bf16[32,256,128]{2,1,0:T(8,128)(2,1)}) custom-call(s32[1,8192]{1,0:T(1,128)} %perm.1, f32[1]{0:T(128)S(6)} %copy.18.rate_ref, f32[32,8192]{1,0:T(8,128)} %pts.1, f32[64,128]{1,0:T(8,128)} %bitcast.7), custom_call_target="tpu_custom_call" | custom-call | tf_op jit(solution)/shard_map/tree_order/pallas_call | solution.py:215
  19.2 30.9 %tree.1 = (f32[32,256]{1,0:T(8,128)}, f32[32,4096]{1,0:T(8,128)}, f32[16,256]{1,0:T(8,128)}, f32[32,4096]{1,0:T(8,128)}, f32[16,256]{1,0:T(8,128)}) custom-call(f32[1]{0:T(128)S(6)} %copy.18.rate_ref, bf16[32,256,128]{2,1,0:T(8,128)(2,1)} %get-tuple-element.16.rows, f32[62,32,256]{2,1,0:T(8,128)} %skel_hbm.1, f32[4,2,32,256]{3,2,1,0:T(8,128)} %skel.1, ...), custom_call_target="tpu_custom_call" | custom-call | tf_op jit(solution)/shard_map/tree/pallas_call | solution.py:457
  50.1 17.6 %near_far.1.image = f32[64,128]{1,0:T(8,128)} custom-call(s32[256]{0:T(256)} %tgt.1, s32[256]{0:T(256)} %src.1, s32[1]{0:T(128)S(6)} %copy.19.cnt, s32[1]{0:T(128)} %bitcast.first_ref, f32[1]{0:T(128)S(6)} %copy.18.rate_ref, f32[1]{0:T(128)S(6)} %copy.17.ridge_ref, s32[32,256]{1,0:T(8,128)} %reshape.31.perm, f32[32,8192]{1,0:T(8,128)} %get-tuple-element.14.gt, ...), custom_call_target="tpu_custom_call" | custom-call | tf_op jit(solution)/shard_map/near_far/pallas_call | solution.py:231
  67.7 21.6 %step.1.factors = f32[16,128]{1,0:T(8,128)} custom-call(f32[64,128]{1,0:T(8,128)} %near_far.1.image, f32[64,128]{1,0:T(8,128)} %bitcast.10, f32[64,128]{1,0:T(8,128)} %bitcast.8), custom_call_target="tpu_custom_call" | custom-call | tf_op jit(solution)/shard_map/step/pallas_call | solution.py:562
  89.3 1.5 %update.1 = (f32[64,128]{1,0:T(8,128)}, f32[64,128]{1,0:T(8,128)}, f32[64,128]{1,0:T(8,128)}) custom-call(f32[16,128]{1,0:T(8,128)} %step.1.factors, f32[64,128]{1,0:T(8,128)} %near_far.1.image, f32[64,128]{1,0:T(8,128)} %bitcast.12, f32[64,128]{1,0:T(8,128)} %bitcast.11, f32[64,128]{1,0:T(8,128)} %bitcast.9), custom_call_target="tpu_custom_call" | custom-call | tf_op jit(solution)/shard_map/update/pallas_call | solution.py:576

commit v5 on v4

--- a/solution.py
+++ b/solution.py
@@ -13,7 +13,7 @@
 REACH = 16
 DIM = 32
 NODES = 62
-WAYS = 8
+WAYS = 16
 SUMS = 2
 
 epsilon = 1e-06
@@ -159,7 +159,7 @@
         return 0
 
     fetch.wait()
-    lax.fori_loop(0, LEAVES_DEV, far, 0, unroll=2)
+    lax.fori_loop(0, LEAVES_DEV, far, 0, unroll=4)
 
     total = cnt[0]
 
@@ -187,14 +187,14 @@
         )
         return 0
 
-    lax.fori_loop(0, LEAVES_DEV, gather_image, 0)
+    lax.fori_loop(0, LEAVES_DEV, gather_image, 0, unroll=2)
     tree_image = turned_img[...].T
 
     grand = jnp.zeros((192, 128), F32)
     high_id = lax.broadcasted_iota(jnp.int32, (64, LEAF), 0)
     low_id = lax.broadcasted_iota(jnp.int32, (128, LEAF), 0)
     for j in range(LEAVES_DEV):
-        at = perm[j : j + 1, :]
+        at = perm[:, j * LEAF : (j + 1) * LEAF]
         value = tree_image[j : j + 1, :] + ridge_ref[0] * dirs[REACH + j][0:1, :]
         hot = high_id == (at >> 7)
         picked = jnp.concatenate(
@@ -608,7 +608,7 @@
     own_first = (lax.axis_index("leaf") * LEAVES_DEV).astype(jnp.int32).reshape(1)
     image = call_down(
         near_target, near_source, tile_count, own_first, kernel_rate, ridge_weight,
-        tree_perm.reshape(LEAVES_DEV, LEAF), gt, own_dir, left, left_dir,
+        tree_perm, gt, own_dir, left, left_dir,
         right, right_dir, rows, down, local_skeleton,
     )
     return tuple(array.reshape(-1) for array in call_step(devices, image, *folded))

time: 90.7 us -> 83.2 us (0.917)
  Pallas kernels: 85.6 us -> 80.8 us
  other arithmetic: 1.48 us -> 0 us
  local copies, waits for them, and re-layouts: 1.14 us -> 0 us
    pallas_call x1, Pallas kernels: 17.6 us -> 13.8 us  [call_down(): pl.pallas_call(down_kernel, out_shape=jax.ShapeDtypeStruct((64, 128), F32...]
    unnamed x1 -> x0, other arithmetic: 1.48 us -> none
    pallas_call x1, Pallas kernels: 21.6 us -> 20.6 us  [call_step(): pl.pallas_call(functools.partial(step_kernel, devices), out_shape=jax.Sha...]
where the time goes in v5:
time: 83.2 us; the launch traced here: 83.4 us
  Pallas kernels  80.8 us (97%)
  between operations  2.6 us (3%)
    pallas_call x1, Pallas kernels, call_cross(): pl.pallas_call(functools.partial(cross_kernel, devices), out_shape=(jax.S...  30.9 us
    pallas_call x1, Pallas kernels, call_step(): pl.pallas_call(functools.partial(step_kernel, devices), out_shape=jax.Sha...  20.6 us
    pallas_call x1, Pallas kernels, call_order(): pl.pallas_call(order_kernel, out_shape=(jax.ShapeDtypeStruct((DIM, count)...  14 us
    pallas_call x1, Pallas kernels, call_down(): pl.pallas_call(down_kernel, out_shape=jax.ShapeDtypeStruct((64, 128), F32...  13.8 us

profile of v5, /device:TPU:0, one launch (start us, length us, event | category | flops | bytes accessed | tf_op | source)
XLA Modules:
  0.0 83.4 jit_solution(804376755273157337)
XLA Ops:
  2.6 14.0 %tree_order.1 = (f32[32,8192]{1,0:T(8,128)}, f32[32,256]{1,0:T(8,128)}, bf16[32,256,128]{2,1,0:T(8,128)(2,1)}) custom-call(s32[1,8192]{1,0:T(1,128)} %perm.3, f32[1]{0:T(128)S(6)} %copy.18.rate_ref, f32[32,8192]{1,0:T(8,128)} %pts.1, f32[64,128]{1,0:T(8,128)} %bitcast.7), custom_call_target="tpu_custom_call" | custom-call | tf_op jit(solution)/shard_map/tree_order/pallas_call | solution.py:215
  16.6 30.9 %tree.1 = (f32[32,256]{1,0:T(8,128)}, f32[32,4096]{1,0:T(8,128)}, f32[16,256]{1,0:T(8,128)}, f32[32,4096]{1,0:T(8,128)}, f32[16,256]{1,0:T(8,128)}) custom-call(f32[1]{0:T(128)S(6)} %copy.18.rate_ref, bf16[32,256,128]{2,1,0:T(8,128)(2,1)} %get-tuple-element.16.rows, f32[62,32,256]{2,1,0:T(8,128)} %skel_hbm.1, f32[4,2,32,256]{3,2,1,0:T(8,128)} %skel.1, ...), custom_call_target="tpu_custom_call" | custom-call | tf_op jit(solution)/shard_map/tree/pallas_call | solution.py:457
  47.5 13.8 %near_far.1.image = f32[64,128]{1,0:T(8,128)} custom-call(s32[256]{0:T(256)} %tgt.1, s32[256]{0:T(256)} %src.1, s32[1]{0:T(128)S(6)} %copy.19.cnt, s32[1]{0:T(128)} %bitcast.first_ref, f32[1]{0:T(128)S(6)} %copy.18.rate_ref, f32[1]{0:T(128)S(6)} %copy.17.ridge_ref, s32[1,8192]{1,0:T(1,128)} %perm.3, f32[32,8192]{1,0:T(8,128)} %get-tuple-element.14.gt, ...), custom_call_target="tpu_custom_call" | custom-call | tf_op jit(solution)/shard_map/near_far/pallas_call | solution.py:231
  61.3 20.6 %step.1.factors = f32[16,128]{1,0:T(8,128)} custom-call(f32[64,128]{1,0:T(8,128)} %near_far.1.image, f32[64,128]{1,0:T(8,128)} %bitcast.10, f32[64,128]{1,0:T(8,128)} %bitcast.8), custom_call_target="tpu_custom_call" | custom-call | tf_op jit(solution)/shard_map/step/pallas_call | solution.py:562
  81.9 1.5 %update.1 = (f32[64,128]{1,0:T(8,128)}, f32[64,128]{1,0:T(8,128)}, f32[64,128]{1,0:T(8,128)}) custom-call(f32[16,128]{1,0:T(8,128)} %step.1.factors, f32[64,128]{1,0:T(8,128)} %near_far.1.image, f32[64,128]{1,0:T(8,128)} %bitcast.12, f32[64,128]{1,0:T(8,128)} %bitcast.11, f32[64,128]{1,0:T(8,128)} %bitcast.9), custom_call_target="tpu_custom_call" | custom-call | tf_op jit(solution)/shard_map/update/pallas_call | solution.py:576
